TPU v7x, 512 devices: a whole 4x8x8 slice. The times are simulated.
512 devices in a mesh: pb: 32 (over y, x), row: 16 (over z, core).
Axes of the slice: x: 4, y: 8, z: 8, core: 2. Of those that a mesh axis runs over, the one named last changes fastest.
Arguments:
- valence_bands: bfloat16 [32, 20, 4096], P('pb', None, 'row'), may hold values from -0.75 to 0.75
- conduction_bands: bfloat16 [32, 20, 4096], P('pb', None, 'row'), may hold values from -6 to 6
- screened: bfloat16 [32, 4096, 4096], P('pb', 'row'), may hold values from -0.09375 to 0.09375
- pair_list: int32 [64, 2], replicated, may hold values from 0 to 31, as said below
- transfer_index: int32 [64, 1], replicated, may hold values from 0 to 31; in each aligned block of 64 rows (0 to 63, 64 to 127, ...) at most 6 rows name the same one
- owner_map: int32 [32], replicated, may hold values from 0 to 31, as said below
Outputs:
- direct: bfloat16 [64, 400, 400], P('pb', 'row')
- mirror: bfloat16 [64, 400, 400], P('pb', 'row')
Inputs may be any that keep to these rules, and one draw needn't show every extreme that they name: owner_map is a permutation of 0 to 31. `pair_list`: the two k-points of a pair differ. The first k-point of pairs e * 2 to e * 2 + 1 is the one that owner_map sends to e. Over all pairs, the second k-points are sent by owner_map to every value 0 to 31 exactly 2 times. `transfer_index`: at most 6 pairs share one momentum transfer, and some transfer has exactly 6; every transfer has at least one pair.
All inputs are finite; a program needn't handle non-finite values.
Results may differ from a plain program's by a relative error of at most 0.0065.
Values may be sent and summed in bfloat16 or wider, within the bound.
A program may use at most 64 MiB of HBM per device.

v0:
```python
import jax
import jax.numpy as jnp
from jax import lax
from jax.sharding import Mesh
from jax.sharding import PartitionSpec as P

PAIR_DEV = 2
MOST = 6
PB = ("pb_0", "pb_1")
ROW = ("row_0", "row_1")


def sent_together(arrays, axis, dim, along):
    ends, at = ([], 0)
    for a in arrays[:-1]:
        at += a.shape[along]
        ends.append(at)
    both = jnp.concatenate(arrays, axis=along)
    return tuple(jnp.split(lax.all_gather(both, axis, axis=dim, tiled=True), ends, axis=along))


def gathered_by_axis(x, axes, dim):
    out = x
    for number in range(len(axes) - 1, -1, -1):
        out = lax.all_gather(out, axes[number], axis=dim, tiled=True)
    return out


def in_blocks(x, dim, peers):
    dims = x.shape
    tiles = x.reshape(*dims[:dim], peers, dims[dim] // peers, *dims[dim + 1 :])
    return jnp.moveaxis(tiles, dim, 0)


def sent_and_summed(x, axis, dim):
    tiles = in_blocks(x, dim, lax.axis_size(axis))
    arrived = lax.all_to_all(tiles, axis, split_axis=0, concat_axis=0, tiled=True)
    return arrived.astype(jnp.float32).sum(axis=0)


def rank_table(labels, groups, slots_per):
    total_rows = labels.shape[0]
    member = (labels[None, :] == jnp.arange(groups, dtype=jnp.int32)[:, None]).astype(jnp.int32)
    before = jnp.cumsum(member, axis=1) - 1
    placed = member[:, None, :] * (
        before[:, None, :] == jnp.arange(slots_per, dtype=jnp.int32)[None, :, None]
    ).astype(jnp.int32)
    numbers = jnp.arange(total_rows, dtype=jnp.int32) + 1
    return jnp.sum(placed * numbers[None, None, :], axis=2) - 1


def pair_kernel(val_first, val_second, con_first, con_second, screen_rows):
    val_count = val_first.shape[0]
    con_count = con_first.shape[0]
    val_pairs = val_first[:, None, :].astype(jnp.float32) * val_second[None, :, :].astype(
        jnp.float32
    )
    val_pairs = val_pairs.reshape(val_count * val_count, val_first.shape[1]).astype(jnp.bfloat16)
    con_pairs = con_first[:, None, :].astype(jnp.float32) * con_second[None, :, :].astype(
        jnp.float32
    )
    con_pairs = con_pairs.reshape(con_count * con_count, con_first.shape[1]).astype(jnp.bfloat16)
    interim = lax.dot_general(
        screen_rows, con_pairs, (((1,), (1,)), ((), ())), preferred_element_type=jnp.float32
    ).astype(jnp.bfloat16)
    partial_sum = jnp.dot(val_pairs, interim, preferred_element_type=jnp.float32)
    partial_sum = partial_sum.reshape(val_count, val_count, con_count, con_count).transpose(
        0, 2, 1, 3
    )
    return partial_sum.reshape(val_count * con_count, val_count * con_count)


def shards(valence_bands, conduction_bands, screened, pair_list, transfer_index, owner_map):
    groups = lax.axis_size(PB)
    rows_split = lax.axis_size(ROW)
    device = lax.axis_index(PB)
    val_all, con_local = sent_together((valence_bands, conduction_bands), PB, 0, 1)
    slot_table = rank_table(transfer_index[:, 0], groups, MOST)
    own_slots = lax.dynamic_index_in_dim(slot_table, device, 0, keepdims=False)
    live_pair = jnp.maximum(own_slots, 0)
    slot_first = jnp.take(owner_map, jnp.take(pair_list[:, 0], live_pair))
    slot_second = jnp.take(owner_map, jnp.take(pair_list[:, 1], live_pair))
    val_first = jnp.take(val_all, slot_first, axis=0)
    val_second = jnp.take(val_all, slot_second, axis=0)
    chosen = jnp.take(con_local, jnp.concatenate([slot_first, slot_second]), axis=0)
    widened = gathered_by_axis(chosen, ROW, 2)
    con_first = widened[:MOST]
    con_second = widened[MOST:]
    screen_rows = screened[0]

    def one_slot(operands):
        return pair_kernel(operands[0], operands[1], operands[2], operands[3], screen_rows)

    partials = lax.map(one_slot, (val_first, val_second, con_first, con_second))
    shares = sent_and_summed(partials.astype(jnp.bfloat16), ROW, 1).astype(jnp.bfloat16)
    band_rows = shares.shape[1]
    mirror_table = rank_table(jnp.take(owner_map, pair_list[:, 1]), groups, PAIR_DEV)
    flat_slots = slot_table.reshape(-1)
    own_direct = device * PAIR_DEV + jnp.arange(PAIR_DEV, dtype=jnp.int32)
    own_mirror = lax.dynamic_index_in_dim(mirror_table, device, 0, keepdims=False)
    wanted = jnp.concatenate([own_direct, own_mirror])
    select = (wanted[:, None] == flat_slots[None, :]).astype(jnp.bfloat16)
    arrived = jnp.einsum(
        "ji,ixy->jxy", select, gathered_by_axis(shares, PB, 0), preferred_element_type=jnp.float32
    )
    direct = arrived[:PAIR_DEV].astype(jnp.bfloat16)
    mirror_rows = arrived[PAIR_DEV:].astype(jnp.bfloat16)
    turned = jnp.transpose(mirror_rows, (0, 2, 1)).reshape(
        PAIR_DEV, rows_split, band_rows, band_rows
    )
    swapped = lax.all_to_all(turned, ROW, split_axis=1, concat_axis=3, tiled=True)
    mirror = swapped.reshape(PAIR_DEV, band_rows, band_rows * rows_split)
    return (direct, mirror)


def solution(mesh):
    split = Mesh(mesh.devices.reshape(8, 4, 8, 2), ("pb_0", "pb_1", "row_0", "row_1"))
    in_specs = (P(PB, None, ROW), P(PB, None, ROW), P(PB, ROW, None), P(), P(), P())
    out_specs = (P(PB, ROW, None), P(PB, ROW, None))
    return jax.shard_map(
        shards, mesh=split, in_specs=in_specs, out_specs=out_specs, check_vma=False
    )
```

profile of v0, /device:TPU:1, one launch (start us, length us, event | category | flops | bytes accessed | tf_op | source)
XLA Modules:
  0.0 385.5 jit_solution(17078036171700090464)
XLA Ops:
  12.9 39.9 %all_gather.15 = bf16[32,40,256]{2,1,0:T(8,128)(2,1)S(1)} all-gather(bf16[1,40,256]{2,1,0:T(8,128)(2,1)S(1)} %pad_maximum_fusion), channel_id=1, replica_groups=mesh['pb_0'=8,'pb_1'=4,'row_0'=8,'row_1'=2] {'pb_0','pb_1'}, dimensions={0}, use_global_device_ids=true | all-gather | bytes 675840 | tf_op jit(solution)/shard_map/all_gather | solution.py:19
  53.6 15.1 %all_gather.16 = bf16[12,20,512]{2,1,0:T(8,128)(2,1)} all-gather(bf16[12,20,256]{2,1,0:T(8,128)(2,1)S(1)} %broadcast_select_fusion), channel_id=1, replica_groups=mesh['pb_0'=8,'pb_1'=4,'row_0'=8,'row_1'=2] {'row_1'}, dimensions={2}, use_global_device_ids=true | all-gather | bytes 368640 | tf_op jit(solution)/shard_map/all_gather | solution.py:25
  71.3 39.5 %all-gather.3.cloned.1.call-done = bf16[12,20,4096]{2,1,0:T(8,128)(2,1)} async-done(((bf16[12,20,512]{2,1,0:T(8,128)(2,1)}), bf16[12,20,4096]{2,1,0:T(8,128)(2,1)}) %all-gather.3.cloned.1.call-update) | async-done | bytes 1966096 | tf_op jit(solution)/shard_map/all_gather | solution.py:25
  110.7 3.3 fusion.12
  114.1 82.8 %while.10 = (s32[]{:T(128)}, bf16[6,400,400]{2,1,0:T(8,128)(2,1)}, bf16[6,20,256]{2,1,0:T(8,128)(2,1)}, bf16[6,20,256]{2,1,0:T(8,128)(2,1)}, bf16[6,20,4096]{2,1...) while((s32[]{:T(128)}, bf16[6,400,400]{2,1,0:T(8,128)(2,1)}, ...), condition=%wide.region_5.9_spmd, body=%wide.region_4.8_spmd.sunk | while | flops 924538880 | bytes 19454556 | solution.py:94
  115.1 2.5 multiply_convert_fusion.3
  117.7 3.9 %convert_element_type.90 = bf16[400,4096]{1,0:T(8,128)(2,1)S(1)} reshape(bf16[20,20,4096]{2,1,0:T(8,128)(2,1)} %multiply_convert_fusion.3) | data formatting | bytes 6553600 | tf_op jit(solution)/shard_map/while/body/eval_jaxpr/convert_element_type | solution.py:62
  121.6 2.6 convolution_convert_fusion.3
  128.9 2.5 multiply_convert_fusion.3
  131.5 3.9 %convert_element_type.90 = bf16[400,4096]{1,0:T(8,128)(2,1)S(1)} reshape(bf16[20,20,4096]{2,1,0:T(8,128)(2,1)} %multiply_convert_fusion.3) | data formatting | bytes 6553600 | tf_op jit(solution)/shard_map/while/body/eval_jaxpr/convert_element_type | solution.py:62
  135.4 2.6 convolution_convert_fusion.3
  142.7 2.5 multiply_convert_fusion.3
  145.3 3.9 %convert_element_type.90 = bf16[400,4096]{1,0:T(8,128)(2,1)S(1)} reshape(bf16[20,20,4096]{2,1,0:T(8,128)(2,1)} %multiply_convert_fusion.3) | data formatting | bytes 6553600 | tf_op jit(solution)/shard_map/while/body/eval_jaxpr/convert_element_type | solution.py:62
  149.2 2.6 convolution_convert_fusion.3
  153.4 1.2 broadcast_in_dim.75
  156.5 2.5 multiply_convert_fusion.3
  159.1 3.9 %convert_element_type.90 = bf16[400,4096]{1,0:T(8,128)(2,1)S(1)} reshape(bf16[20,20,4096]{2,1,0:T(8,128)(2,1)} %multiply_convert_fusion.3) | data formatting | bytes 6553600 | tf_op jit(solution)/shard_map/while/body/eval_jaxpr/convert_element_type | solution.py:62
  163.0 2.6 convolution_convert_fusion.3
  167.2 1.2 broadcast_in_dim.75
  170.3 2.5 multiply_convert_fusion.3
  172.9 3.9 %convert_element_type.90 = bf16[400,4096]{1,0:T(8,128)(2,1)S(1)} reshape(bf16[20,20,4096]{2,1,0:T(8,128)(2,1)} %multiply_convert_fusion.3) | data formatting | bytes 6553600 | tf_op jit(solution)/shard_map/while/body/eval_jaxpr/convert_element_type | solution.py:62
  176.8 2.6 convolution_convert_fusion.3
  181.0 1.2 broadcast_in_dim.75
  184.2 2.5 multiply_convert_fusion.3
  186.7 3.9 %convert_element_type.90 = bf16[400,4096]{1,0:T(8,128)(2,1)S(1)} reshape(bf16[20,20,4096]{2,1,0:T(8,128)(2,1)} %multiply_convert_fusion.3) | data formatting | bytes 6553600 | tf_op jit(solution)/shard_map/while/body/eval_jaxpr/convert_element_type | solution.py:62
  190.6 2.6 convolution_convert_fusion.3
  196.9 2.9 reshape.263
  200.0 81.6 %all_to_all.20 = bf16[16,6,25,400]{3,2,1,0:T(8,128)(2,1)S(1)} all-to-all(bf16[16,6,25,400]{3,2,1,0:T(8,128)(2,1)S(1)} %copy.22), channel_id=1, replica_groups=mesh['pb_0'=8,'pb_1'=4,'row_0'=8,'row_1'=2] {'row_0','row_1'}, dimensions={0} | all-to-all | bytes 3840000 | tf_op jit(solution)/shard_map/all_to_all | solution.py:37
  282.2 13.1 %all_gather.18 = bf16[24,25,400]{2,1,0:T(8,128)(2,1)S(1)} all-gather(bf16[6,25,400]{2,1,0:T(8,128)(2,1)S(1)} %reduce_sum.32), channel_id=1, replica_groups=mesh['pb_0'=8,'pb_1'=4,'row_0'=8,'row_1'=2] {'pb_1'}, dimensions={0}, use_global_device_ids=true | all-gather | bytes 600000 | tf_op jit(solution)/shard_map/all_gather | solution.py:25
  298.2 59.5 %all-gather.5.cloned.1.call-done = bf16[192,25,400]{2,0,1:T(8,128)(2,1)} async-done(((bf16[24,25,400]{2,0,1:T(8,128)(2,1)}), bf16[192,25,400]{2,0,1:T(8,128)(2,1)}) %all-gather.5.cloned.1.call-update) | async-done | bytes 3840016 | tf_op jit(solution)/shard_map/all_gather | solution.py:25
  357.7 3.2 convolution_convert_fusion.1
  362.3 15.3 %all_to_all.21 = bf16[16,2,625]{2,1,0:T(2,128)(2,1)S(1)} all-to-all(bf16[16,2,625]{2,1,0:T(2,128)(2,1)S(1)} %reshape.358), channel_id=1, replica_groups=mesh['pb_0'=8,'pb_1'=4,'row_0'=8,'row_1'=2] {'row_0','row_1'}, dimensions={0} | all-to-all | bytes 80000 | tf_op jit(solution)/shard_map/all_to_all | solution.py:111
  (97 shorter events, 39.6 us)
Async XLA Ops:
  7.2 3.5 copy-start
  7.2 103.6 %all-gather.3.cloned.1.call-start = ((), (), s32[]{:S(2)}) async-start(), calls=%async_computation.2 | async-start | bytes 2654208 | tf_op jit(solution)/shard_map/all_gather | solution.py:25
  68.7 289.0 %all-gather.5.cloned.1.call-start = ((), (), s32[]{:S(2)}) async-start(), calls=%async_computation.3 | async-start | bytes 5529600 | tf_op jit(solution)/shard_map/all_gather | solution.py:25
  282.2 15.2 %copy-start.1 = (s32[64,2]{0,1:T(2,128)S(1)}, s32[64,2]{0,1:T(2,128)}, u32[]{:S(2)}) copy-start(s32[64,2]{0,1:T(2,128)} %param.17) | copy-start | bytes 1540
Sparse Core Ops, SparseCore 0:
  68.8 41.9 all-gather.2
  296.6 60.9 all-gather.4
where the time goes:
time: 387 us; the launch traced here: 385 us
  blocking collectives  165 us (43%)
  waiting for transfers between devices  99 us (26%)
  local copies, waits for them, and re-layouts  51.4 us (13%)
  other arithmetic  31.7 us (8%)
  matrix products  23.9 us (6%)
  between operations  14.3 us (4%)
    all_gather x2, waiting for transfers between devices, gathered_by_axis(): out = lax.all_gather(out, axes[number], axis=dim, tiled=True)  99 us
    all_to_all x1, blocking collectives, sent_and_summed(): lax.all_to_all(tiles, axis, split_axis=0, concat_axis=0, tiled=True)  81.6 us
    all_gather x1, blocking collectives, sent_together(): lax.all_gather(both, axis, axis=dim, tiled=True)  39.9 us
    all_gather x2, blocking collectives, gathered_by_axis(): out = lax.all_gather(out, axes[number], axis=dim, tiled=True)  28.1 us
    convert_element_type x6, local copies, waits for them, and re-layouts, pair_kernel(): con_pairs.reshape(con_count * con_count, con_first.shape[1])  23.3 us
    dot_general x6, matrix products, pair_kernel(): lax.dot_general(screen_rows, con_pairs, (((1,), (1,)), ((), ())), preferr...  15.8 us
    all_to_all x1, blocking collectives, shards(): lax.all_to_all(turned, ROW, split_axis=1, concat_axis=3, tiled=True)  15.3 us
    convert_element_type x6, other arithmetic, pair_kernel(): con_pairs.reshape(con_count * con_count, con_first.shape[1])  15.3 us
  transfers between devices with their start and end apart: 2, of which 2 were waited for; matrix products, arithmetic and copies ran while one was open for 1% of the time, Pallas kernels for 0%

commit v1 on v0

v1 whole, which is shorter than its diff:
```python
import functools

import jax
import jax.numpy as jnp
import numpy as np
from jax import lax
from jax.experimental import pallas as pl
from jax.experimental.pallas import tpu as pltpu
from jax.sharding import Mesh
from jax.sharding import PartitionSpec as P

MESH = pl.DeviceIdType.MESH
BF = jnp.bfloat16
F32 = jnp.float32
NB = 20
BP = 24
KB = 2 * BP
CG = 4
CW = NB // CG
PAIR_DEV = 2
MOST = 6
HALF = MOST // 2


def up(n, to):
    return -(-n // to) * to


def kernel(
    ny, nx, nz,
    tab, val, con, w_any, spread_d, mask_d, spread_m, mask_m, collect,
    out_d, out_m,
    w, call, vall, g, acc, prod, valp, pf, pp, rr, rp, rm, sp, sm, yb, xs, xr, ms, mr,
    bar_w, s_c, r_c, s_v, r_v,
    gs_p, gr_p, gs_m, gr_m, ss_s, ss_r,
    p_s, p_r, qs_p, qr_p, qs_m, qr_m,
    ys_p, yr_p, ys_m, yr_m, xs_s, xs_r, ms_s, ms_r,
):
    y, x, z, c = (lax.axis_index(a) for a in ("y", "x", "z", "c"))
    npb = ny * nx
    rows = 2 * nz
    me = y * nx + x
    row = z * 2 + c
    share = NB * NB // rows
    units = NB * CG // rows

    def at_pb(e):
        return (e // nx, lax.rem(e, nx), z, c)

    def at_row(r):
        return (y, x, r // 2, lax.rem(r, 2))

    def zrel(k):
        return lax.rem(z + k + 2 * nz, nz)

    def yrel(k):
        return lax.rem(y + k + 2 * ny, ny)

    barrier = pltpu.get_barrier_semaphore()

    @pl.loop(1, npb)
    def _(i):
        pl.semaphore_signal(barrier, inc=1, device_id=at_pb(lax.rem(me + i, npb)), device_id_type=MESH)

    @pl.loop(1, rows)
    def _(i):
        pl.semaphore_signal(barrier, inc=1, device_id=at_row(lax.rem(row + i, rows)), device_id_type=MESH)

    get_w = pltpu.make_async_copy(w_any.at[0], w, bar_w)
    get_w.start()

    def stage(buf, src):
        blank = jnp.zeros((BP - NB, 128), BF)
        for h in range(2):
            part = src[0, :, h * 128:(h + 1) * 128]
            buf[me, h * BP:(h + 1) * BP, :] = jnp.concatenate([part, blank], axis=0)

    stage(call, con)
    stage(vall, val)
    pl.semaphore_wait(barrier, npb - 1 + rows - 1)

    for buf, s_sem, r_sem in ((call, s_c, r_c), (vall, s_v, r_v)):
        @pl.loop(1, npb)
        def _(i, buf=buf, s_sem=s_sem, r_sem=r_sem):
            pltpu.make_async_remote_copy(
                src_ref=buf.at[me], dst_ref=buf.at[me], send_sem=s_sem, recv_sem=r_sem,
                device_id=at_pb(lax.rem(me + i, npb)), device_id_type=MESH,
            ).start()

    def all_of(buf, sem):
        ref = buf.at[pl.ds(0, npb - 1)]
        pltpu.make_async_copy(ref, ref, sem).wait()

    pf[:, units * NB:, :] = jnp.zeros((rows, pf.shape[1] - units * NB, 128), F32)

    @pl.loop(0, MOST)
    def _(s):
        acc[s] = jnp.zeros(acc.shape[1:], F32)

    all_of(call, r_c)

    @pl.loop(0, 2 * MOST)
    def _(i):
        g[row, i] = call[tab[me * 2 * MOST + i]]

    def gsend(d, t):
        r = zrel(-d * (t - 1)) * 2 + c
        blk = g.at[r]
        if t == nz // 2:
            blk = g.at[r, pl.ds(0 if d > 0 else MOST, MOST)]
        s_sem, r_sem = (gs_p, gr_p) if d > 0 else (gs_m, gr_m)
        return pltpu.make_async_remote_copy(
            src_ref=blk, dst_ref=blk, send_sem=s_sem.at[t - 1], recv_sem=r_sem.at[t - 1],
            device_id=(y, x, zrel(d), c), device_id_type=MESH,
        )

    def grecv(d, t):
        r = zrel(-d * t) * 2 + c
        blk = g.at[r]
        if t == nz // 2:
            blk = g.at[r, pl.ds(0 if d > 0 else MOST, MOST)]
        pltpu.make_async_copy(blk, blk, (gr_p if d > 0 else gr_m).at[t - 1]).wait()

    def sibling(zz, core):
        blk = g.at[zz * 2 + core]
        return pltpu.make_async_remote_copy(
            src_ref=blk, dst_ref=blk, send_sem=ss_s.at[zz], recv_sem=ss_r.at[zz],
            device_id=(y, x, z, 1 - c), device_id_type=MESH,
        )

    def block(zz):
        @pl.loop(0, MOST)
        def _(s):
            for core in range(2):
                for h in range(2):
                    lane = (core * 2 + h) * 128
                    one = g[zz * 2 + core, s, h * BP:(h + 1) * BP, :]
                    two = g[zz * 2 + core, MOST + s, h * BP:(h + 1) * BP, :]
                    for k in range(NB):
                        prod[k * BP:(k + 1) * BP, lane:lane + 128] = one[k:k + 1, :] * two
            cols = pl.ds(pl.multiple_of(zz * 512, 512), 512)
            acc[s] += lax.dot_general(
                prod[...], w[:, cols], (((1,), (1,)), ((), ())), preferred_element_type=F32
            )

    top = nz // 2
    gsend(1, 1).start()
    gsend(-1, 1).start()
    sibling(z, c).start()
    get_w.wait()
    for t in range(1, top + 1):
        if t == 1:
            sibling(z, 1 - c).wait_recv()
            block(z)
        elif t == top and top > 1:
            pass
        grecv(1, t)
        grecv(-1, t)
        if t < top:
            gsend(1, t + 1).start()
            gsend(-1, t + 1).start()
            sibling(zrel(-t), c).start()
            sibling(zrel(t), c).start()
        else:
            sibling(zrel(t), c).start()
        for k in ((-t, t) if t < top else (t,)):
            sibling(zrel(k), 1 - c).wait_recv()
            block(zrel(k))

    all_of(vall, r_v)

    @pl.loop(0, MOST)
    def _(s):
        one = vall[tab[me * 2 * MOST + s]]
        two = vall[tab[me * 2 * MOST + MOST + s]]
        for h in range(2):
            a, b = one[h * BP:(h + 1) * BP, :], two[h * BP:(h + 1) * BP, :]
            for k in range(NB):
                valp[k * BP:(k + 1) * BP, h * 128:(h + 1) * 128] = a[k:k + 1, :] * b
        for q in range(CG):
            it = jnp.concatenate(
                [acc[s, (q * CW + k) * BP:(q * CW + k) * BP + NB, :] for k in range(CW)]
                + [jnp.zeros((128 - CW * NB, 256), F32)], axis=0,
            ).astype(BF)
            part = lax.dot_general(valp[...], it, (((1,), (1,)), ((), ())), preferred_element_type=F32)
            for v in range(NB):
                u = v * CG + q
                r, i = u // units, u % units
                pf[r, i * NB:(i + 1) * NB, :] = part[v * BP:v * BP + NB, :]
        for r in range(rows):
            pp[s, r % 2, r // 2] = pf[r].astype(BF)
        pltpu.make_async_remote_copy(
            src_ref=pp.at[s, 1 - c], dst_ref=rr.at[s], send_sem=p_s.at[s], recv_sem=p_r.at[s],
            device_id=(y, x, z, 1 - c), device_id_type=MESH,
        ).start()

    def pair_copy(s):
        return pltpu.make_async_remote_copy(
            src_ref=pp.at[s, 1 - c], dst_ref=rr.at[s], send_sem=p_s.at[s], recv_sem=p_r.at[s],
            device_id=(y, x, z, 1 - c), device_id_type=MESH,
        )

    def qsend(d, t, s):
        out, into, s_sem, r_sem = (sp, rp, qs_p, qr_p) if d > 0 else (sm, rm, qs_m, qr_m)
        return pltpu.make_async_remote_copy(
            src_ref=out.at[t - 1, s], dst_ref=into.at[t - 1, s],
            send_sem=s_sem.at[t - 1, s], recv_sem=r_sem.at[t - 1, s],
            device_id=(y, x, zrel(d), c), device_id_type=MESH,
        )

    def first_half(d):
        return (0, HALF) if d > 0 else (HALF, MOST)

    def qstep(d, t, s, add):
        out, into = (sp, rp) if d > 0 else (sm, rm)
        own = pp[s, c, zrel(d * (top + 1 - t))]
        if add:
            qsend(d, t - 1, s).wait_recv()
            own = (own.astype(F32) + into[t - 2, s].astype(F32)).astype(BF)
        out[t - 1, s] = own
        qsend(d, t, s).start()

    def has(d, t, s):
        return t > 1 or first_half(d)[0] <= s < first_half(d)[1]

    for s in range(MOST):
        pair_copy(s).wait_recv()
        for zz in range(nz):
            pp[s, c, zz] = (pp[s, c, zz].astype(F32) + rr[s, zz].astype(F32)).astype(BF)
        for d in (1, -1):
            if has(d, 1, s):
                qstep(d, 1, s, False)
    for t in range(2, top + 1):
        for s in range(MOST):
            for d in (1, -1):
                qstep(d, t, s, has(d, t - 1, s))

    ytop = ny // 2

    def ysend(d, t, s):
        blk = yb.at[yrel(-d * (t - 1)), s]
        s_sem, r_sem = (ys_p, yr_p) if d > 0 else (ys_m, yr_m)
        return pltpu.make_async_remote_copy(
            src_ref=blk, dst_ref=blk, send_sem=s_sem.at[t - 1, s], recv_sem=r_sem.at[t - 1, s],
            device_id=(yrel(d), x, z, c), device_id_type=MESH,
        )

    def yhas(d, t, s):
        return t < ytop or first_half(d)[0] <= s < first_half(d)[1]

    def yrecv(d, t, s):
        blk = yb.at[yrel(-d * t), s]
        pltpu.make_async_copy(blk, blk, (yr_p if d > 0 else yr_m).at[t - 1, s]).wait()

    for s in range(MOST):
        total = pp[s, c, z].astype(F32)
        for d, into in ((1, rp), (-1, rm)):
            if has(d, top, s):
                qsend(d, top, s).wait_recv()
                total = total + into[top - 1, s].astype(F32)
        yb[y, s] = total.astype(BF)
        for d in (1, -1):
            if yhas(d, 1, s):
                ysend(d, 1, s).start()
    for t in range(1, ytop + 1):
        for s in range(MOST):
            for d in (1, -1):
                if yhas(d, t, s):
                    yrecv(d, t, s)
                    if t < ytop and yhas(d, t + 1, s):
                        ysend(d, t + 1, s).start()

    base = 2 * MOST * npb

    def xcopy(i):
        to = lax.rem(x + i, nx)
        return pltpu.make_async_remote_copy(
            src_ref=xs.at[to], dst_ref=xr.at[x], send_sem=xs_s.at[i], recv_sem=xs_r.at[i],
            device_id=(y, to, z, c), device_id_type=MESH,
        )

    for i in range(nx):
        to = lax.rem(x + i, nx)
        dest = xr if i == 0 else xs
        for j in range(2 * PAIR_DEV):
            pick = tab[base + (y * nx + to) * 4 + j]
            slot = tab[base + 4 * npb + (y * nx + to) * 4 + j]
            dest[to, j] = yb[pick, slot]
        if i:
            xcopy(i).start()
    for i in range(1, nx):
        xcopy(i).wait_recv()

    srows = xs.shape[2]
    at_r = lax.broadcasted_iota(jnp.int32, (srows, 128), 0)
    at_l = lax.broadcasted_iota(jnp.int32, (srows, 128), 1)

    def ordered(j, spread, mask):
        got = xr[tab[base + 8 * npb + me * 4 + j], j].astype(F32)
        kept = [
            jnp.where((at_r < units * NB) & (at_l >= k * NB) & (at_l < (k + 1) * NB), got, 0.0).astype(BF)
            for k in range(CW)
        ]
        parts = []
        for k in range(CW):
            wide = jnp.dot(kept[k], spread[...], preferred_element_type=F32)
            parts.append((wide * mask[...].astype(F32)).astype(BF))
        return jnp.dot(collect[...], jnp.concatenate(parts, axis=0), preferred_element_type=F32)

    rpad = up(share, 32)
    turned = jnp.concatenate(
        [ordered(PAIR_DEV + j, spread_m, mask_m) for j in range(PAIR_DEV)]
        + [jnp.zeros((128 - PAIR_DEV * rpad, rows * rpad), F32)], axis=0,
    ).T.astype(BF)
    for r in range(rows):
        ms[r] = turned[r * rpad:(r + 1) * rpad, :]
    mr[row] = ms[row]

    def mcopy(i):
        to = lax.rem(row + i, rows)
        return pltpu.make_async_remote_copy(
            src_ref=ms.at[to], dst_ref=mr.at[row], send_sem=ms_s.at[i], recv_sem=ms_r.at[i],
            device_id=at_row(to), device_id_type=MESH,
        )

    @pl.loop(1, rows)
    def _(i):
        mcopy(i).start()

    for j in range(PAIR_DEV):
        out_d[j] = ordered(j, spread_d, mask_d)[:share, :NB * NB].astype(BF)

    @pl.loop(1, rows)
    def _(i):
        mcopy(i).wait_recv()

    for j in range(PAIR_DEV):
        out_m[j] = jnp.concatenate(
            [mr[r].astype(F32)[:share, j * rpad:j * rpad + share] for r in range(rows)], axis=1
        ).astype(BF)

    all_of(call, s_c)
    all_of(vall, s_v)
    for t in range(1, top + 1):
        gsend(1, t).wait_send()
        gsend(-1, t).wait_send()
    for k in range(nz):
        sibling(k, c).wait_send()
    for s in range(MOST):
        pair_copy(s).wait_send()
        for t in range(1, top + 1):
            for d in (1, -1):
                if has(d, t, s):
                    qsend(d, t, s).wait_send()
        for t in range(1, ytop + 1):
            for d in (1, -1):
                if yhas(d, t, s):
                    ysend(d, t, s).wait_send()
    for i in range(1, nx):
        xcopy(i).wait_send()

    @pl.loop(1, rows)
    def _(i):
        mcopy(i).wait_send()


def constants(rows):
    share = NB * NB // rows
    units = NB * CG // rows
    srows = up(units * NB, 16)
    rpad = up(share, 32)
    lane = np.arange(128)
    plain = np.arange(up(NB * NB, 128))
    wd = np.where(plain < NB * NB, plain, -1)
    padded = np.arange(rows * rpad)
    wdm = np.where(padded % rpad < share, padded // rpad * share + padded % rpad, -1)
    r = np.arange(srows)

    def two(cols):
        spread = (lane[:, None] < CW * NB) & (cols[None, :] >= 0) & (lane[:, None] % NB == cols[None, :] % NB)
        mask = (r[:, None] < units * NB) & (cols[None, :] >= 0) & (r[:, None] % NB == cols[None, :] // NB)
        return spread, mask

    k = np.arange(CW * srows)
    out = np.arange(rpad)
    rr = k % srows
    collect = (
        (rr[None, :] < units * NB) & (out[:, None] < share)
        & (rr[None, :] // NB == out[:, None] // CW) & (k[None, :] // srows == out[:, None] % CW)
    )
    return [a.astype(np.float32).astype(BF) for a in (*two(wd), *two(wdm), collect)]


def table(pair_list, transfer_index, owner_map, npb):
    i32 = jnp.int32
    n = pair_list.shape[0]
    t = transfer_index[:, 0]
    p = jnp.arange(n, dtype=i32)
    ks = jnp.arange(owner_map.shape[0], dtype=i32)

    def owner(k):
        return jnp.sum(jnp.where(k[:, None] == ks[None, :], owner_map[None, :], 0), axis=1)

    def rank(labels):
        same = (labels[:, None] == labels[None, :]) & (p[None, :] < p[:, None])
        return jnp.sum(same.astype(i32), axis=1)

    first, second = owner(pair_list[:, 0]), owner(pair_list[:, 1])
    place = rank(t)
    q = jnp.arange(npb, dtype=i32)
    hit = (t[None, None, :] == q[:, None, None]) & (
        place[None, None, :] == jnp.arange(MOST, dtype=i32)[None, :, None]
    )
    one = jnp.sum(jnp.where(hit, first[None, None, :], 0), axis=2)
    two = jnp.sum(jnp.where(hit, second[None, None, :], 0), axis=2)
    j = jnp.arange(PAIR_DEV, dtype=i32)
    code = t * MOST + place
    hit_m = (second[None, None, :] == q[:, None, None]) & (rank(second)[None, None, :] == j[None, :, None])
    mirrored = jnp.sum(jnp.where(hit_m, code[None, None, :], 0), axis=2)
    want = jnp.concatenate([code.reshape(npb, PAIR_DEV), mirrored], axis=1)
    return one, two, want


def solution(mesh):
    sizes = tuple(int(np.prod([mesh.shape[a]])) for a in ("pb", "row"))
    nx, ny, nz = GRID.get(sizes, (4, 8, 8))
    split = Mesh(mesh.devices.reshape(ny, nx, nz, 2), ("y", "x", "z", "c"))
    npb, rows = ny * nx, 2 * nz
    share, units = NB * NB // rows, NB * CG // rows
    srows, rpad = up(units * NB, 16), up(share, 32)
    top, ytop = nz // 2, ny // 2
    dma = pltpu.SemaphoreType.DMA

    def shards(val, con, screened, pair_list, transfer_index, owner_map):
        one, two, want = table(pair_list, transfer_index, owner_map, npb)
        tab = jnp.concatenate([
            jnp.concatenate([one, two], axis=1).reshape(-1),
            (want // MOST // nx).reshape(-1), (want % MOST).reshape(-1), (want // MOST % nx).reshape(-1),
        ])
        consts = [jnp.asarray(a) for a in constants(rows)]
        vmem = pl.BlockSpec(memory_space=pltpu.VMEM)
        points = screened.shape[2]
        blk = (srows, 128)
        scratch = [
            pltpu.VMEM((256, points), BF),
            pltpu.VMEM((npb, KB, 128), BF),
            pltpu.VMEM((npb, KB, 128), BF),
            pltpu.VMEM((rows, 2 * MOST, KB, 128), BF),
            pltpu.VMEM((MOST, NB * BP, 256), F32),
            pltpu.VMEM((NB * BP, 512), BF),
            pltpu.VMEM((NB * BP, 256), BF),
            pltpu.VMEM((rows, *blk), F32),
            pltpu.VMEM((MOST, 2, nz, *blk), BF),
            pltpu.VMEM((MOST, nz, *blk), BF),
            *[pltpu.VMEM((top, MOST, *blk), BF) for _ in range(4)],
            pltpu.VMEM((ny, MOST, *blk), BF),
            pltpu.VMEM((nx, 4, *blk), BF),
            pltpu.VMEM((nx, 4, *blk), BF),
            pltpu.VMEM((rows, rpad, 128), BF),
            pltpu.VMEM((rows, rpad, 128), BF),
            dma, dma, dma, dma, dma,
            *[dma((top,)) for _ in range(4)],
            dma((nz,)), dma((nz,)),
            dma((MOST,)), dma((MOST,)),
            *[dma((top, MOST)) for _ in range(4)],
            *[dma((ytop, MOST)) for _ in range(4)],
            dma((nx,)), dma((nx,)), dma((rows,)), dma((rows,)),
        ]
        result = jax.ShapeDtypeStruct((PAIR_DEV, share, NB * NB), BF)
        return pl.pallas_call(
            functools.partial(kernel, ny, nx, nz),
            out_shape=(result, result),
            in_specs=[pl.BlockSpec(memory_space=pltpu.SMEM), vmem, vmem,
                      pl.BlockSpec(memory_space=pl.ANY), *[vmem] * 5],
            out_specs=(vmem, vmem),
            scratch_shapes=scratch,
            compiler_params=pltpu.CompilerParams(
                collective_id=0, has_side_effects=True, vmem_limit_bytes=50 * 2**20
            ),
        )(tab, val, con, screened, *consts)

    in_specs = (P(("y", "x"), None, ("z", "c")), P(("y", "x"), None, ("z", "c")),
                P(("y", "x"), ("z", "c"), None), P(), P(), P())
    out = P(("y", "x"), ("z", "c"), None)
    return jax.shard_map(shards, mesh=split, in_specs=in_specs, out_specs=(out, out), check_vma=False)


GRID = {(4, 4): (2, 2, 2), (2, 8): (1, 2, 4)}
```

time: 387 us -> 120 us (0.31)
  blocking collectives: 165 us -> 0 us
  Pallas kernels: 0 us -> 103 us
  waiting for transfers between devices: 99 us -> 0 us
  local copies, waits for them, and re-layouts: 51.4 us -> 10.6 us
  other arithmetic: 31.7 us -> 4.34 us
  matrix products: 23.9 us -> 0 us
  between operations: 14.3 us -> 0.74 us
    pallas_call x0 -> x1, Pallas kernels: none -> 103 us  [shards(): pl.pallas_call(functools.partial(kernel, ny, nx, nz), out_shape=(result,...]
    all_gather x2 -> x0, waiting for transfers between devices: 99 us -> none  [gathered_by_axis(): out = lax.all_gather(out, axes[number], axis=dim, tiled=True)]
    all_to_all x2 -> x0, blocking collectives: 96.8 us -> none  [the longest x1 81.6 us: sent_and_summed(): lax.all_to_all(tiles, axis, split_axis=0, concat_axis=0, tiled=True)]
    all_gather x3 -> x0, blocking collectives: 68 us -> none  [the longest x1 39.9 us: sent_together(): lax.all_gather(both, axis, axis=dim, tiled=True)]
    dot_general x13 -> x0, matrix products: 23.9 us -> none  [the longest x6 15.8 us: pair_kernel(): lax.dot_general(screen_rows, con_pairs, (((1,), (1,)), ((), ())), preferr...]
    convert_element_type x6 -> x0, local copies, waits for them, and re-layouts: 23.3 us -> none  [pair_kernel(): con_pairs.reshape(con_count * con_count, con_first.shape[1])]
    convert_element_type x8 -> x0, other arithmetic: 15.9 us -> none  [the longest x6 15.3 us: pair_kernel(): con_pairs.reshape(con_count * con_count, con_first.shape[1])]
    mul x12 -> x1, other arithmetic: 10.9 us -> 0.67 us  [table(): code = t * MOST + place]
  transfers between devices with their start and end apart: 2 -> 0, of which waited for: 2 -> 0; matrix products, arithmetic and copies ran while one was open for 1% -> 0% of each run, Pallas kernels for 0% -> 0%
where the time goes in v1:
time: 120 us; the launch traced here: 119 us
  Pallas kernels  103 us (86%)
  local copies, waits for them, and re-layouts  10.6 us (9%)
  other arithmetic  4.34 us (4%)
    pallas_call x1, Pallas kernels, shards(): pl.pallas_call(functools.partial(kernel, ny, nx, nz), out_shape=(result,...  103 us
    unnamed x16, local copies, waits for them, and re-layouts  7.38 us

profile of v1, /device:TPU:1, one launch (start us, length us, event | category | flops | bytes accessed | tf_op | source)
XLA Modules:
  0.0 119.1 jit_solution(3582197435083307934)
XLA Ops:
  0.6 0.9 convert_reduce_fusion.1
  1.5 0.7 multiply_add_fusion
  2.2 0.7 multiply_reduce_fusion
  2.9 0.8 slice_bitcast_fusion
  3.6 0.7 select_reduce_fusion.2
  4.4 0.2 convert_reduce_fusion
  4.6 0.1 select_reduce_fusion
  4.7 0.7 iota_compare_fusion.4
  5.4 0.3 fusion
  5.7 0.1 copy.23
  5.8 0.1 reshape.131
  5.9 0.1 reduce_sum.70
  6.0 0.1 mul.20
  6.1 0.1 copy.24
  6.2 0.1 copy.25
  6.3 0.1 ne.54
  6.4 0.1 copy.26
  6.5 0.1 rem.45
  6.6 0.1 copy.27
  6.7 0.1 div.24
  6.9 0.0 copy-start
  6.9 1.6 %copy-done = bf16[1,256,4096]{2,1,0:T(8,128)(2,1)S(1)} copy-done((bf16[1,256,4096]{2,1,0:T(8,128)(2,1)S(1)}, bf16[1,256,4096]{2,1,0:T(8,128)(2,1)}, u32[]{:S(2)}) %copy-start) | copy-done | bytes 2097176
  8.5 0.9 copy-done.1
  9.4 0.9 copy-done.2
  10.3 0.9 copy-done.3
  11.2 0.9 copy-done.4
  12.1 0.8 copy-done.5
  12.9 0.7 copy-done.6
  13.6 0.7 copy-done.7
  14.3 103.5 %shard_map.122 = (bf16[2,25,400]{2,1,0:T(8,128)(2,1)S(1)}, bf16[2,25,400]{2,1,0:T(8,128)(2,1)S(1)}) custom-call(s32[768]{0:T(1024)S(1)} %pad_add_fusion.1.tab, bf16[1,20,256]{2,1,0:T(8,128)(2,1)S(1)} %copy-done.6, bf16[1,20,256]{2,1,0:T(8,128)(2,1)S(1)} %copy-done.7, bf16[1,256,4096]{2,1,0:T(8,128)(2,1)S(1)} %copy-done, bf16[128,512]{1,0:T(8,128)(2,1)S(1)} %copy-done.2, ...), custom_call_target="tpu_custom_call" | custom-call | tf_op jit(solution)/shard_map/pallas_call | solution.py:470
  117.8 0.7 copy.28
  118.5 0.7 copy.29
  (17 shorter events, 0.1 us)
Async XLA Ops:
  6.9 1.6 %copy-start = (bf16[1,256,4096]{2,1,0:T(8,128)(2,1)S(1)}, bf16[1,256,4096]{2,1,0:T(8,128)(2,1)}, u32[]{:S(2)}) copy-start(bf16[1,256,4096]{2,1,0:T(8,128)(2,1)} %w_any.1) | copy-start | bytes 6291460
  8.5 0.9 copy-start.1
  9.4 0.9 copy-start.2
  10.3 0.9 copy-start.3
  11.2 0.9 copy-start.4
  12.1 0.8 copy-start.5
  12.9 0.7 copy-start.6
  13.6 0.7 copy-start.7

commit v2 on v1

v2 whole, which is shorter than its diff:
```python
import functools

import jax
import jax.numpy as jnp
import numpy as np
from jax import lax
from jax.experimental import pallas as pl
from jax.experimental.pallas import tpu as pltpu
from jax.sharding import Mesh
from jax.sharding import PartitionSpec as P

MESH = pl.DeviceIdType.MESH
BF = jnp.bfloat16
F32 = jnp.float32
NB = 20
BP = 24
KB = 2 * BP
CG = 4
CW = NB // CG
PAIR_DEV = 2
MOST = 6
HALF = MOST // 2


def up(n, to):
    return -(-n // to) * to


def kernel(
    ny, nx, nz, pairs,
    tab, val_any, con_any, w_any, spread_d_any, mask_d_any, spread_m_any, mask_m_any, collect_any,
    out_d, out_m,
    val, con, w, spread_d, mask_d, spread_m, mask_m, collect,
    call, vall, g, acc, prod, valp, pf, pp, rr, rp, rm, sp, sm, yb, xs, xr_d, xr_m, ms, mr,
    loc_t, loc,
    bx_s, bx_r, bs_p, br_p, bs_m, br_m,
    gs_p, gr_p, gs_m, gr_m, ss_s, ss_r,
    p_s, p_r, qs_p, qr_p, qs_m, qr_m,
    ys_p, yr_p, ys_m, yr_m, xs_s, xs_r, ms_s, ms_r,
):
    y, x, z, c = (lax.axis_index(a) for a in ("y", "x", "z", "c"))
    rows = 2 * nz
    me = y * nx + x
    row = z * 2 + c
    share = NB * NB // rows
    units = NB * CG // rows
    top, ytop = nz // 2, ny // 2

    def at_row(r):
        return (y, x, r // 2, lax.rem(r, 2))

    def zrel(k):
        return lax.rem(z + k + 2 * nz, nz)

    def yrel(k):
        return lax.rem(y + k + 2 * ny, ny)

    def xrel(k):
        return lax.rem(x + k + 2 * nx, nx)

    barrier = pltpu.get_barrier_semaphore()
    for i in range(1, nx):
        pl.semaphore_signal(barrier, inc=1, device_id=(y, xrel(i), z, c), device_id_type=MESH)
    for d in (1, -1):
        pl.semaphore_signal(barrier, inc=1, device_id=(yrel(d), x, z, c), device_id_type=MESH)

    @pl.loop(1, rows)
    def _(i):
        pl.semaphore_signal(barrier, inc=1, device_id=at_row(lax.rem(row + i, rows)), device_id_type=MESH)

    fetch = [
        pltpu.make_async_copy(a, b, loc.at[i])
        for i, (a, b) in enumerate((
            (con_any, con), (val_any, val), (w_any.at[0], w), (spread_d_any, spread_d), (mask_d_any, mask_d),
            (spread_m_any, spread_m), (mask_m_any, mask_m), (collect_any, collect),
        ))
    ]
    for f in fetch:
        f.start()

    def stage(buf, src):
        blank = jnp.zeros((BP - NB, 128), BF)
        for h in range(2):
            part = src[0, :, h * 128:(h + 1) * 128]
            buf[y, x, h * BP:(h + 1) * BP, :] = jnp.concatenate([part, blank], axis=0)

    fetch[0].wait()
    stage(call, con)
    fetch[1].wait()
    stage(vall, val)
    pl.semaphore_wait(barrier, nx - 1 + 2 + rows - 1)

    def bx(n, i):
        ref = (call, vall)[n].at[y, x]
        return pltpu.make_async_remote_copy(
            src_ref=ref, dst_ref=ref, send_sem=bx_s.at[n, i], recv_sem=bx_r.at[n, i],
            device_id=(y, xrel(i), z, c), device_id_type=MESH,
        )

    def bx_recv(n, i):
        ref = (call, vall)[n].at[y, xrel(-i)]
        pltpu.make_async_copy(ref, ref, bx_r.at[n, i]).wait()

    def b_has(d, t, i):
        return t < ytop or (i < nx // 2 if d > 0 else i >= nx // 2)

    def by(n, d, t, i):
        ref = (call, vall)[n].at[yrel(-d * (t - 1)), xrel(-i)]
        s_sem, r_sem = (bs_p, br_p) if d > 0 else (bs_m, br_m)
        return pltpu.make_async_remote_copy(
            src_ref=ref, dst_ref=ref, send_sem=s_sem.at[n, t - 1, i], recv_sem=r_sem.at[n, t - 1, i],
            device_id=(yrel(d), x, z, c), device_id_type=MESH,
        )

    def by_recv(n, d, t, i):
        ref = (call, vall)[n].at[yrel(-d * t), xrel(-i)]
        pltpu.make_async_copy(ref, ref, (br_p if d > 0 else br_m).at[n, t - 1, i]).wait()

    def by_first(n):
        for i in range(nx):
            if i:
                bx_recv(n, i)
            for d in (1, -1):
                if b_has(d, 1, i):
                    by(n, d, 1, i).start()

    def by_step(n, t):
        for i in range(nx):
            for d in (1, -1):
                if b_has(d, t, i):
                    by_recv(n, d, t, i)
                    if t < ytop and b_has(d, t + 1, i):
                        by(n, d, t + 1, i).start()

    for n in range(2):
        for i in range(1, nx):
            bx(n, i).start()
    by_first(0)

    pf[:, units * NB:, :] = jnp.zeros((rows, pf.shape[1] - units * NB, 128), F32)

    @pl.loop(0, MOST)
    def _(s):
        acc[s] = jnp.zeros(acc.shape[1:], F32)

    def owner(k):
        return tab[3 * pairs + k]

    def own_slots(p, carry):
        count, slots = carry
        hit = tab[p] == me
        slots = tuple(jnp.where(hit & (count == s), p, slots[s]) for s in range(MOST))
        return count + hit.astype(jnp.int32), slots

    zero = jnp.int32(0)
    _, slots = lax.fori_loop(0, pairs, own_slots, (zero, (zero,) * MOST))
    first = [owner(tab[pairs + p]) for p in slots]
    second = [owner(tab[2 * pairs + p]) for p in slots]

    def by_second(p, carry):
        e = owner(tab[2 * pairs + p])
        new = []
        for k in range(nx):
            count, one, two = carry[k]
            hit = e == y * nx + k
            new.append((count + hit.astype(jnp.int32), jnp.where(hit & (count == 0), p, one),
                        jnp.where(hit & (count == 1), p, two)))
        return tuple(new)

    found = lax.fori_loop(0, pairs, by_second, ((zero,) * 3,) * nx)
    wanted = []
    for k in range(nx):
        at = (y * nx + k) * PAIR_DEV
        wanted += [at, at + 1, found[k][1], found[k][2]]
    column = [tab[p] for p in wanted]

    def ranks(p, carry):
        return tuple(
            n + ((tab[p] == q) & (p < own)).astype(jnp.int32) for n, q, own in zip(carry, column, wanted)
        )

    ranked = lax.fori_loop(0, pairs, ranks, (zero,) * len(wanted))
    for i in range(4 * nx):
        loc_t[i] = lax.div(column[i], nx)
        loc_t[4 * nx + i] = jnp.minimum(ranked[i], MOST - 1)
        loc_t[8 * nx + i] = lax.rem(column[i], nx)

    for t in range(1, ytop + 1):
        by_step(0, t)

    for i, k in enumerate(first + second):
        g[row, i] = call[lax.div(k, nx), lax.rem(k, nx)]

    def g_has(d, t, h):
        return t < top or h == (0 if d > 0 else 1)

    def g_ref(k, h):
        return g.at[zrel(k) * 2 + c, pl.ds(h * MOST, MOST)]

    def gsend(d, t, h):
        ref = g_ref(-d * (t - 1), h)
        s_sem, r_sem = (gs_p, gr_p) if d > 0 else (gs_m, gr_m)
        return pltpu.make_async_remote_copy(
            src_ref=ref, dst_ref=ref, send_sem=s_sem.at[t - 1, h], recv_sem=r_sem.at[t - 1, h],
            device_id=(y, x, zrel(d), c), device_id_type=MESH,
        )

    def grecv(d, t, h):
        ref = g_ref(-d * t, h)
        pltpu.make_async_copy(ref, ref, (gr_p if d > 0 else gr_m).at[t - 1, h]).wait()

    def sibling(zz, core, h):
        ref = g.at[zz * 2 + core, pl.ds(h * MOST, MOST)]
        return pltpu.make_async_remote_copy(
            src_ref=ref, dst_ref=ref, send_sem=ss_s.at[zz, h], recv_sem=ss_r.at[zz, h],
            device_id=(y, x, z, 1 - c), device_id_type=MESH,
        )

    def block(zz):
        for h in range(2):
            sibling(zz, 1 - c, h).wait_recv()

        @pl.loop(0, MOST)
        def _(s):
            for core in range(2):
                for h in range(2):
                    lane = (core * 2 + h) * 128
                    one = g[zz * 2 + core, s, h * BP:(h + 1) * BP, :]
                    two = g[zz * 2 + core, MOST + s, h * BP:(h + 1) * BP, :]
                    for k in range(NB):
                        prod[k * BP:(k + 1) * BP, lane:lane + 128] = one[k:k + 1, :] * two
            cols = pl.ds(pl.multiple_of(zz * 512, 512), 512)
            acc[s] += lax.dot_general(
                prod[...], w[:, cols], (((1,), (1,)), ((), ())), preferred_element_type=F32
            )

    for h in range(2):
        for d in (1, -1):
            if g_has(d, 1, h):
                gsend(d, 1, h).start()
        sibling(z, c, h).start()
    by_first(1)
    fetch[2].wait()
    before = [z]
    for t in range(1, top + 1):
        for h in range(2):
            for d in (1, -1):
                if g_has(d, t, h):
                    grecv(d, t, h)
                    if t < top and g_has(d, t + 1, h):
                        gsend(d, t + 1, h).start()
                    sibling(zrel(-d * t), c, h).start()
            if h < len(before):
                block(before[h])
        before = [zrel(-t), zrel(t)] if t < top else [zrel(t)]
        if t <= ytop:
            by_step(1, t)
    for t in range(top + 1, ytop + 1):
        by_step(1, t)
    for zz in before:
        block(zz)

    def pair_copy(s):
        return pltpu.make_async_remote_copy(
            src_ref=pp.at[s, 1 - c], dst_ref=rr.at[s], send_sem=p_s.at[s], recv_sem=p_r.at[s],
            device_id=(y, x, z, 1 - c), device_id_type=MESH,
        )

    def partial(s):
        one = vall[lax.div(first[s], nx), lax.rem(first[s], nx)]
        two = vall[lax.div(second[s], nx), lax.rem(second[s], nx)]
        for h in range(2):
            a, b = one[h * BP:(h + 1) * BP, :], two[h * BP:(h + 1) * BP, :]
            for k in range(NB):
                valp[k * BP:(k + 1) * BP, h * 128:(h + 1) * 128] = a[k:k + 1, :] * b
        for q in range(CG):
            it = jnp.concatenate(
                [acc[s, (q * CW + k) * BP:(q * CW + k) * BP + NB, :] for k in range(CW)]
                + [jnp.zeros((128 - CW * NB, 256), F32)], axis=0,
            ).astype(BF)
            part = lax.dot_general(valp[...], it, (((1,), (1,)), ((), ())), preferred_element_type=F32)
            for v in range(NB):
                u = v * CG + q
                r, i = u // units, u % units
                pf[r, i * NB:(i + 1) * NB, :] = part[v * BP:v * BP + NB, :]
        for r in range(rows):
            pp[s, r % 2, r // 2] = pf[r].astype(BF)
        pair_copy(s).start()

    def qsend(d, t, s):
        out, into, s_sem, r_sem = (sp, rp, qs_p, qr_p) if d > 0 else (sm, rm, qs_m, qr_m)
        return pltpu.make_async_remote_copy(
            src_ref=out.at[t - 1, s], dst_ref=into.at[t - 1, s],
            send_sem=s_sem.at[t - 1, s], recv_sem=r_sem.at[t - 1, s],
            device_id=(y, x, zrel(d), c), device_id_type=MESH,
        )

    def first_half(d):
        return (0, HALF) if d > 0 else (HALF, MOST)

    def has(d, t, s):
        return t > 1 or first_half(d)[0] <= s < first_half(d)[1]

    def qstep(d, t, s, add):
        out, into = (sp, rp) if d > 0 else (sm, rm)
        own = pp[s, c, zrel(d * (top + 1 - t))]
        if add:
            qsend(d, t - 1, s).wait_recv()
            own = (own.astype(F32) + into[t - 2, s].astype(F32)).astype(BF)
        out[t - 1, s] = own
        qsend(d, t, s).start()

    def added(s):
        pair_copy(s).wait_recv()

        @pl.loop(0, nz)
        def _(zz):
            pp[s, c, zz] = (pp[s, c, zz].astype(F32) + rr[s, zz].astype(F32)).astype(BF)

        for d in (1, -1):
            if has(d, 1, s):
                qstep(d, 1, s, False)
            elif top > 1:
                qstep(d, 2, s, False)

    def ysend(d, t, s):
        blk = yb.at[yrel(-d * (t - 1)), s]
        s_sem, r_sem = (ys_p, yr_p) if d > 0 else (ys_m, yr_m)
        return pltpu.make_async_remote_copy(
            src_ref=blk, dst_ref=blk, send_sem=s_sem.at[t - 1, s], recv_sem=r_sem.at[t - 1, s],
            device_id=(yrel(d), x, z, c), device_id_type=MESH,
        )

    def yhas(d, t, s):
        return t < ytop or first_half(d)[0] <= s < first_half(d)[1]

    def yrecv(d, t, s):
        blk = yb.at[yrel(-d * t), s]
        pltpu.make_async_copy(blk, blk, (yr_p if d > 0 else yr_m).at[t - 1, s]).wait()

    def done(s):
        total = pp[s, c, z].astype(F32)
        for d, into in ((1, rp), (-1, rm)):
            if has(d, top, s):
                qsend(d, top, s).wait_recv()
                total = total + into[top - 1, s].astype(F32)
        yb[y, s] = total.astype(BF)
        for d in (1, -1):
            if yhas(d, 1, s):
                ysend(d, 1, s).start()

    def ystep(t, s):
        for d in (1, -1):
            if yhas(d, t, s):
                yrecv(d, t, s)
                if t < ytop and yhas(d, t + 1, s):
                    ysend(d, t + 1, s).start()

    stages = [partial, added]
    for t in range(2, top + 1):
        def stage_q(s, t=t):
            for d in (1, -1):
                if t > 2 or has(d, 1, s):
                    qstep(d, t, s, True)
        stages.append(stage_q)
    stages.append(done)
    for t in range(1, ytop + 1):
        stages.append(functools.partial(ystep, t))
    for step in range(MOST + len(stages) - 1):
        for k in reversed(range(len(stages))):
            if 0 <= step - k < MOST:
                stages[k](step - k)

    def xcopy(i, m):
        to = xrel(i)
        part = pl.ds(m * PAIR_DEV, PAIR_DEV)
        return pltpu.make_async_remote_copy(
            src_ref=xs.at[to, part], dst_ref=(xr_d, xr_m)[m].at[x], send_sem=xs_s.at[m, i], recv_sem=xs_r.at[m, i],
            device_id=(y, to, z, c), device_id_type=MESH,
        )

    for m in (1, 0):
        for i in list(range(1, nx)) + [0]:
            to = xrel(i)
            for j in range(m * PAIR_DEV, (m + 1) * PAIR_DEV):
                got = yb[loc_t[to * 4 + j], loc_t[4 * nx + to * 4 + j]]
                if i:
                    xs[to, j] = got
                else:
                    (xr_d, xr_m)[m][to, j - m * PAIR_DEV] = got
            if i:
                xcopy(i, m).start()

    for f in fetch[3:]:
        f.wait()
    for i in range(1, nx):
        xcopy(i, 1).wait_recv()

    srows = xs.shape[2]
    at_r = lax.broadcasted_iota(jnp.int32, (srows, 128), 0)
    at_l = lax.broadcasted_iota(jnp.int32, (srows, 128), 1)

    def ordered(m, j, spread, mask):
        got = (xr_d, xr_m)[m][loc_t[8 * nx + x * 4 + m * PAIR_DEV + j], j].astype(F32)
        kept = [
            jnp.where((at_r < units * NB) & (at_l >= k * NB) & (at_l < (k + 1) * NB), got, 0.0).astype(BF)
            for k in range(CW)
        ]
        parts = []
        for k in range(CW):
            wide = jnp.dot(kept[k], spread[...], preferred_element_type=F32)
            parts.append((wide * mask[...].astype(F32)).astype(BF))
        return jnp.dot(collect[...], jnp.concatenate(parts, axis=0), preferred_element_type=F32)

    rpad = up(share, 32)
    turned = jnp.concatenate(
        [ordered(1, j, spread_m, mask_m) for j in range(PAIR_DEV)]
        + [jnp.zeros((128 - PAIR_DEV * rpad, rows * rpad), F32)], axis=0,
    ).T.astype(BF)
    for r in range(rows):
        ms[r] = turned[r * rpad:(r + 1) * rpad, :]
    mr[row] = ms[row]

    def mcopy(i):
        to = lax.rem(row + i, rows)
        return pltpu.make_async_remote_copy(
            src_ref=ms.at[to], dst_ref=mr.at[row], send_sem=ms_s.at[i], recv_sem=ms_r.at[i],
            device_id=at_row(to), device_id_type=MESH,
        )

    @pl.loop(1, rows)
    def _(i):
        mcopy(i).start()

    for i in range(1, nx):
        xcopy(i, 0).wait_recv()
    for j in range(PAIR_DEV):
        out_d[j] = ordered(0, j, spread_d, mask_d)[:share, :NB * NB].astype(BF)

    @pl.loop(1, rows)
    def _(i):
        mcopy(i).wait_recv()

    for j in range(PAIR_DEV):
        out_m[j] = jnp.concatenate(
            [mr[r].astype(F32)[:share, j * rpad:j * rpad + share] for r in range(rows)], axis=1
        ).astype(BF)

    for n in range(2):
        for i in range(1, nx):
            bx(n, i).wait_send()
        for t in range(1, ytop + 1):
            for i in range(nx):
                for d in (1, -1):
                    if b_has(d, t, i):
                        by(n, d, t, i).wait_send()
    for h in range(2):
        for t in range(1, top + 1):
            for d in (1, -1):
                if g_has(d, t, h):
                    gsend(d, t, h).wait_send()
        for k in range(nz):
            sibling(k, c, h).wait_send()
    for s in range(MOST):
        pair_copy(s).wait_send()
        for t in range(1, top + 1):
            for d in (1, -1):
                if has(d, t, s):
                    qsend(d, t, s).wait_send()
        for t in range(1, ytop + 1):
            for d in (1, -1):
                if yhas(d, t, s):
                    ysend(d, t, s).wait_send()
    for m in range(2):
        for i in range(1, nx):
            xcopy(i, m).wait_send()

    @pl.loop(1, rows)
    def _(i):
        mcopy(i).wait_send()


def constants(rows):
    share = NB * NB // rows
    units = NB * CG // rows
    srows = up(units * NB, 16)
    rpad = up(share, 32)
    lane = np.arange(128)
    plain = np.arange(up(NB * NB, 128))
    wd = np.where(plain < NB * NB, plain, -1)
    padded = np.arange(rows * rpad)
    wdm = np.where(padded % rpad < share, padded // rpad * share + padded % rpad, -1)
    r = np.arange(srows)

    def two(cols):
        spread = (lane[:, None] < CW * NB) & (cols[None, :] >= 0) & (lane[:, None] % NB == cols[None, :] % NB)
        mask = (r[:, None] < units * NB) & (cols[None, :] >= 0) & (r[:, None] % NB == cols[None, :] // NB)
        return spread, mask

    k = np.arange(CW * srows)
    out = np.arange(rpad)
    rr = k % srows
    collect = (
        (rr[None, :] < units * NB) & (out[:, None] < share)
        & (rr[None, :] // NB == out[:, None] // CW) & (k[None, :] // srows == out[:, None] % CW)
    )
    return [a.astype(np.float32).astype(BF) for a in (*two(wd), *two(wdm), collect)]


def solution(mesh):
    sizes = tuple(int(np.prod([mesh.shape[a]])) for a in ("pb", "row"))
    nx, ny, nz = GRID.get(sizes, (4, 8, 8))
    split = Mesh(mesh.devices.reshape(ny, nx, nz, 2), ("y", "x", "z", "c"))
    npb, rows = ny * nx, 2 * nz
    share, units = NB * NB // rows, NB * CG // rows
    srows, rpad = up(units * NB, 16), up(share, 32)
    top, ytop = nz // 2, ny // 2
    dma = pltpu.SemaphoreType.DMA

    def shards(val, con, screened, pair_list, transfer_index, owner_map):
        pairs = pair_list.shape[0]
        tab = jnp.concatenate([transfer_index[:, 0], pair_list[:, 0], pair_list[:, 1], owner_map])
        consts = [jnp.asarray(a) for a in constants(rows)]
        vmem, anywhere = pl.BlockSpec(memory_space=pltpu.VMEM), pl.BlockSpec(memory_space=pl.ANY)
        points = screened.shape[2]
        blk = (srows, 128)
        scratch = [
            pltpu.VMEM(val.shape, BF), pltpu.VMEM(con.shape, BF),
            pltpu.VMEM((256, points), BF),
            *[pltpu.VMEM(a.shape, BF) for a in consts],
            pltpu.VMEM((ny, nx, KB, 128), BF),
            pltpu.VMEM((ny, nx, KB, 128), BF),
            pltpu.VMEM((rows, 2 * MOST, KB, 128), BF),
            pltpu.VMEM((MOST, NB * BP, 256), F32),
            pltpu.VMEM((NB * BP, 512), BF),
            pltpu.VMEM((NB * BP, 256), BF),
            pltpu.VMEM((rows, *blk), F32),
            pltpu.VMEM((MOST, 2, nz, *blk), BF),
            pltpu.VMEM((MOST, nz, *blk), BF),
            *[pltpu.VMEM((top, MOST, *blk), BF) for _ in range(4)],
            pltpu.VMEM((ny, MOST, *blk), BF),
            pltpu.VMEM((nx, 2 * PAIR_DEV, *blk), BF),
            pltpu.VMEM((nx, PAIR_DEV, *blk), BF),
            pltpu.VMEM((nx, PAIR_DEV, *blk), BF),
            pltpu.VMEM((rows, rpad, 128), BF),
            pltpu.VMEM((rows, rpad, 128), BF),
            pltpu.SMEM((12 * nx,), jnp.int32),
            dma((8,)),
            dma((2, nx)), dma((2, nx)),
            *[dma((2, ytop, nx)) for _ in range(4)],
            *[dma((top, 2)) for _ in range(4)],
            dma((nz, 2)), dma((nz, 2)),
            dma((MOST,)), dma((MOST,)),
            *[dma((top, MOST)) for _ in range(4)],
            *[dma((ytop, MOST)) for _ in range(4)],
            dma((2, nx)), dma((2, nx)), dma((rows,)), dma((rows,)),
        ]
        result = jax.ShapeDtypeStruct((PAIR_DEV, share, NB * NB), BF)
        return pl.pallas_call(
            functools.partial(kernel, ny, nx, nz, pairs),
            out_shape=(result, result),
            in_specs=[pl.BlockSpec(memory_space=pltpu.SMEM), *[anywhere] * 8],
            out_specs=(vmem, vmem),
            scratch_shapes=scratch,
            compiler_params=pltpu.CompilerParams(
                collective_id=0, has_side_effects=True, vmem_limit_bytes=60 * 2**20
            ),
        )(tab, val, con, screened, *consts)

    in_specs = (P(("y", "x"), None, ("z", "c")), P(("y", "x"), None, ("z", "c")),
                P(("y", "x"), ("z", "c"), None), P(), P(), P())
    out = P(("y", "x"), ("z", "c"), None)
    return jax.shard_map(shards, mesh=split, in_specs=in_specs, out_specs=(out, out), check_vma=False)


GRID = {(4, 4): (2, 2, 2), (2, 8): (1, 2, 4)}
```

time: 120 us -> 127 us (1.058)
  Pallas kernels: 103 us -> 121 us
  local copies, waits for them, and re-layouts: 10.6 us -> 3.79 us
  other arithmetic: 4.34 us -> 1.31 us
    pallas_call x1, Pallas kernels: 103 us -> 121 us  [shards(): pl.pallas_call(functools.partial(kernel, ny, nx, nz, pairs), out_shape=(r...]
    unnamed x16 -> x0, local copies, waits for them, and re-layouts: 7.38 us -> none
    reduce_sum x5 -> x0, other arithmetic: 2.23 us -> none  [the longest x2 1.08 us: rank(): return jnp.sum(same.astype(i32), axis=1)]
    pallas_call x2, local copies, waits for them, and re-layouts: 1.35 us -> 3.03 us  [shards(): pl.pallas_call(functools.partial(kernel, ny, nx, nz, pairs), out_shape=(r...]
    concatenate x2 -> x1, other arithmetic: 0.02 us -> 1.31 us  [shards(): jnp.concatenate([transfer_index[:, 0], pair_list[:, 0], pair_list[:, 1],...]
where the time goes in v2:
time: 127 us; the launch traced here: 126 us
  Pallas kernels  121 us (95%)
  local copies, waits for them, and re-layouts  3.79 us (3%)
  other arithmetic  1.31 us (1%)
    pallas_call x1, Pallas kernels, shards(): pl.pallas_call(functools.partial(kernel, ny, nx, nz, pairs), out_shape=(r...  121 us
    pallas_call x2, local copies, waits for them, and re-layouts, shards(): pl.pallas_call(functools.partial(kernel, ny, nx, nz, pairs), out_shape=(r...  3.03 us

profile of v2, /device:TPU:1, one launch (start us, length us, event | category | flops | bytes accessed | tf_op | source)
XLA Modules:
  0.0 126.5 jit_solution(10554129228638348131)
XLA Ops:
  0.6 0.8 slice_bitcast_fusion.1
  1.4 1.3 %pad_add_fusion.tab = s32[224]{0:T(256)} fusion(s32[32]{0:T(128)} %param.16, s32[64]{0:T(128)S(1)} %get-tuple-element.5, s32[64]{0:T(128)S(1)} %get-tuple-element.4, s32[64]{0:T(128)} %bitcast.5), kind=kLoop, calls=%fused_computation | loop fusion | flops 672 | bytes 1792 | tf_op jit(solution)/shard_map/concatenate | solution.py:522
  2.7 120.7 %shard_map.122 = (bf16[2,25,400]{2,1,0:T(8,128)(2,1)}, bf16[2,25,400]{2,1,0:T(8,128)(2,1)}) custom-call(s32[224]{0:T(256)} %pad_add_fusion.tab, bf16[1,20,256]{2,1,0:T(8,128)(2,1)} %val_any.1, bf16[1,20,256]{2,1,0:T(8,128)(2,1)} %con_any.1, bf16[1,256,4096]{2,1,0:T(8,128)(2,1)} %w_any.1, bf16[128,512]{1,0:T(8,128)(2,1)} %constant.10.clone.spread_d_any, ...), custom_call_target="tpu_custom_call" | custom-call | tf_op jit(solution)/shard_map/pallas_call | solution.py:559
  123.4 1.5 %copy.13 = bf16[2,25,400]{2,0,1:T(2,128)(2,1)} copy(bf16[2,25,400]{2,1,0:T(8,128)(2,1)} %get-tuple-element.2) | data formatting | bytes 80000 | tf_op jit(solution)/shard_map/pallas_call | solution.py:559
  125.0 1.5 %copy.14 = bf16[2,25,400]{2,0,1:T(2,128)(2,1)} copy(bf16[2,25,400]{2,1,0:T(8,128)(2,1)} %get-tuple-element.3) | data formatting | bytes 80000 | tf_op jit(solution)/shard_map/pallas_call | solution.py:559

commit v3 on v2

--- a/solution.py
+++ b/solution.py
@@ -20,6 +20,7 @@
 PAIR_DEV = 2
 MOST = 6
 HALF = MOST // 2
+CHUNKS = 4
 
 
 def up(n, to):
@@ -33,7 +34,7 @@
     val, con, w, spread_d, mask_d, spread_m, mask_m, collect,
     call, vall, g, acc, prod, valp, pf, pp, rr, rp, rm, sp, sm, yb, xs, xr_d, xr_m, ms, mr,
     loc_t, loc,
-    bx_s, bx_r, bs_p, br_p, bs_m, br_m,
+    by_s, by_r, bx_s, bx_r,
     gs_p, gr_p, gs_m, gr_m, ss_s, ss_r,
     p_s, p_r, qs_p, qr_p, qs_m, qr_m,
     ys_p, yr_p, ys_m, yr_m, xs_s, xs_r, ms_s, ms_r,
@@ -61,8 +62,8 @@
     barrier = pltpu.get_barrier_semaphore()
     for i in range(1, nx):
         pl.semaphore_signal(barrier, inc=1, device_id=(y, xrel(i), z, c), device_id_type=MESH)
-    for d in (1, -1):
-        pl.semaphore_signal(barrier, inc=1, device_id=(yrel(d), x, z, c), device_id_type=MESH)
+    for i in range(1, ny):
+        pl.semaphore_signal(barrier, inc=1, device_id=(yrel(i), x, z, c), device_id_type=MESH)
 
     @pl.loop(1, rows)
     def _(i):
@@ -88,60 +89,52 @@
     stage(call, con)
     fetch[1].wait()
     stage(vall, val)
-    pl.semaphore_wait(barrier, nx - 1 + 2 + rows - 1)
-
-    def bx(n, i):
+    pl.semaphore_wait(barrier, nx - 1 + ny - 1 + rows - 1)
+
+    near = sorted(range(1, ny), key=lambda i: min(i, ny - i))
+
+    def by(n, i):
         ref = (call, vall)[n].at[y, x]
         return pltpu.make_async_remote_copy(
-            src_ref=ref, dst_ref=ref, send_sem=bx_s.at[n, i], recv_sem=bx_r.at[n, i],
-            device_id=(y, xrel(i), z, c), device_id_type=MESH,
-        )
-
-    def bx_recv(n, i):
-        ref = (call, vall)[n].at[y, xrel(-i)]
-        pltpu.make_async_copy(ref, ref, bx_r.at[n, i]).wait()
-
-    def b_has(d, t, i):
-        return t < ytop or (i < nx // 2 if d > 0 else i >= nx // 2)
-
-    def by(n, d, t, i):
-        ref = (call, vall)[n].at[yrel(-d * (t - 1)), xrel(-i)]
-        s_sem, r_sem = (bs_p, br_p) if d > 0 else (bs_m, br_m)
-        return pltpu.make_async_remote_copy(
-            src_ref=ref, dst_ref=ref, send_sem=s_sem.at[n, t - 1, i], recv_sem=r_sem.at[n, t - 1, i],
-            device_id=(yrel(d), x, z, c), device_id_type=MESH,
-        )
-
-    def by_recv(n, d, t, i):
-        ref = (call, vall)[n].at[yrel(-d * t), xrel(-i)]
-        pltpu.make_async_copy(ref, ref, (br_p if d > 0 else br_m).at[n, t - 1, i]).wait()
-
-    def by_first(n):
-        for i in range(nx):
-            if i:
-                bx_recv(n, i)
-            for d in (1, -1):
-                if b_has(d, 1, i):
-                    by(n, d, 1, i).start()
-
-    def by_step(n, t):
-        for i in range(nx):
-            for d in (1, -1):
-                if b_has(d, t, i):
-                    by_recv(n, d, t, i)
-                    if t < ytop and b_has(d, t + 1, i):
-                        by(n, d, t + 1, i).start()
-
+            src_ref=ref, dst_ref=ref, send_sem=by_s.at[n, i], recv_sem=by_r.at[n, i],
+            device_id=(yrel(i), x, z, c), device_id_type=MESH,
+        )
+
+    def bx(n, i, k):
+        ref = (call, vall)[n].at[yrel(-i), x]
+        return pltpu.make_async_remote_copy(
+            src_ref=ref, dst_ref=ref, send_sem=bx_s.at[n, i, k], recv_sem=bx_r.at[n, i, k],
+            device_id=(y, xrel(k), z, c), device_id_type=MESH,
+        )
+
+    def b_arrived(n, i, k):
+        ref = (call, vall)[n].at[yrel(-i), xrel(-k)]
+        pltpu.make_async_copy(ref, ref, bx_r.at[n, i, k] if k else by_r.at[n, i]).wait()
+
+    def pass_on(n, i):
+        if i:
+            b_arrived(n, i, 0)
+        for k in range(1, nx):
+            bx(n, i, k).start()
+
+    def all_arrived(n):
+        for i in [0] + near:
+            for k in range(1, nx):
+                b_arrived(n, i, k)
+
+    pass_on(0, 0)
     for n in range(2):
-        for i in range(1, nx):
-            bx(n, i).start()
-    by_first(0)
+        for i in near:
+            by(n, i).start()
 
     pf[:, units * NB:, :] = jnp.zeros((rows, pf.shape[1] - units * NB, 128), F32)
 
     @pl.loop(0, MOST)
     def _(s):
         acc[s] = jnp.zeros(acc.shape[1:], F32)
+
+    for i in near:
+        pass_on(0, i)
 
     def owner(k):
         return tab[3 * pairs + k]
@@ -185,17 +178,18 @@
         loc_t[4 * nx + i] = jnp.minimum(ranked[i], MOST - 1)
         loc_t[8 * nx + i] = lax.rem(column[i], nx)
 
-    for t in range(1, ytop + 1):
-        by_step(0, t)
+    for i in [0] + near:
+        pass_on(1, i)
+    all_arrived(0)
 
     for i, k in enumerate(first + second):
         g[row, i] = call[lax.div(k, nx), lax.rem(k, nx)]
 
     def g_has(d, t, h):
-        return t < top or h == (0 if d > 0 else 1)
+        return t < top or (h < CHUNKS // 2) == (d > 0)
 
     def g_ref(k, h):
-        return g.at[zrel(k) * 2 + c, pl.ds(h * MOST, MOST)]
+        return g.at[zrel(k) * 2 + c, pl.ds(h * (2 * MOST // CHUNKS), 2 * MOST // CHUNKS)]
 
     def gsend(d, t, h):
         ref = g_ref(-d * (t - 1), h)
@@ -234,31 +228,32 @@
                 prod[...], w[:, cols], (((1,), (1,)), ((), ())), preferred_element_type=F32
             )
 
-    for h in range(2):
+    for h in range(CHUNKS):
         for d in (1, -1):
             if g_has(d, 1, h):
                 gsend(d, 1, h).start()
+    for h in range(2):
         sibling(z, c, h).start()
-    by_first(1)
     fetch[2].wait()
     before = [z]
     for t in range(1, top + 1):
-        for h in range(2):
+        for h in range(CHUNKS):
             for d in (1, -1):
                 if g_has(d, t, h):
                     grecv(d, t, h)
                     if t < top and g_has(d, t + 1, h):
                         gsend(d, t + 1, h).start()
-                    sibling(zrel(-d * t), c, h).start()
-            if h < len(before):
-                block(before[h])
+            if (h + 1) % (CHUNKS // 2) == 0:
+                half = (h + 1) // (CHUNKS // 2) - 1
+                for d in (1, -1):
+                    if g_has(d, t, h):
+                        sibling(zrel(-d * t), c, half).start()
+                if half < len(before):
+                    block(before[half])
         before = [zrel(-t), zrel(t)] if t < top else [zrel(t)]
-        if t <= ytop:
-            by_step(1, t)
-    for t in range(top + 1, ytop + 1):
-        by_step(1, t)
     for zz in before:
         block(zz)
+    all_arrived(1)
 
     def pair_copy(s):
         return pltpu.make_async_remote_copy(
@@ -356,20 +351,21 @@
                 if t < ytop and yhas(d, t + 1, s):
                     ysend(d, t + 1, s).start()
 
-    stages = [partial, added]
+    for s in range(MOST + 1):
+        if s < MOST:
+            partial(s)
+        if s:
+            added(s - 1)
     for t in range(2, top + 1):
-        def stage_q(s, t=t):
+        for s in range(MOST):
             for d in (1, -1):
                 if t > 2 or has(d, 1, s):
                     qstep(d, t, s, True)
-        stages.append(stage_q)
-    stages.append(done)
+    for s in range(MOST):
+        done(s)
     for t in range(1, ytop + 1):
-        stages.append(functools.partial(ystep, t))
-    for step in range(MOST + len(stages) - 1):
-        for k in reversed(range(len(stages))):
-            if 0 <= step - k < MOST:
-                stages[k](step - k)
+        for s in range(MOST):
+            ystep(t, s)
 
     def xcopy(i, m):
         to = xrel(i)
@@ -447,19 +443,18 @@
         ).astype(BF)
 
     for n in range(2):
-        for i in range(1, nx):
-            bx(n, i).wait_send()
-        for t in range(1, ytop + 1):
-            for i in range(nx):
-                for d in (1, -1):
-                    if b_has(d, t, i):
-                        by(n, d, t, i).wait_send()
-    for h in range(2):
-        for t in range(1, top + 1):
+        for i in range(ny):
+            if i:
+                by(n, i).wait_send()
+            for k in range(1, nx):
+                bx(n, i, k).wait_send()
+    for t in range(1, top + 1):
+        for h in range(CHUNKS):
             for d in (1, -1):
                 if g_has(d, t, h):
                     gsend(d, t, h).wait_send()
-        for k in range(nz):
+    for k in range(nz):
+        for h in range(2):
             sibling(k, c, h).wait_send()
     for s in range(MOST):
         pair_copy(s).wait_send()
@@ -546,9 +541,8 @@
             pltpu.VMEM((rows, rpad, 128), BF),
             pltpu.SMEM((12 * nx,), jnp.int32),
             dma((8,)),
-            dma((2, nx)), dma((2, nx)),
-            *[dma((2, ytop, nx)) for _ in range(4)],
-            *[dma((top, 2)) for _ in range(4)],
+            dma((2, ny)), dma((2, ny)), dma((2, ny, nx)), dma((2, ny, nx)),
+            *[dma((top, CHUNKS)) for _ in range(4)],
             dma((nz, 2)), dma((nz, 2)),
             dma((MOST,)), dma((MOST,)),
             *[dma((top, MOST)) for _ in range(4)],

time: 127 us -> 107 us (0.84)
  Pallas kernels: 121 us -> 101 us
    pallas_call x1, Pallas kernels: 121 us -> 101 us  [shards(): pl.pallas_call(functools.partial(kernel, ny, nx, nz, pairs), out_shape=(r...]
where the time goes in v3:
time: 107 us
  Pallas kernels  101 us (94%)
  local copies, waits for them, and re-layouts  3.79 us (4%)
  other arithmetic  1.31 us (1%)
    pallas_call x1, Pallas kernels, shards(): pl.pallas_call(functools.partial(kernel, ny, nx, nz, pairs), out_shape=(r...  101 us
    pallas_call x2, local copies, waits for them, and re-layouts, shards(): pl.pallas_call(functools.partial(kernel, ny, nx, nz, pairs), out_shape=(r...  3.03 us

profile of v3, /device:TPU:1, one launch (start us, length us, event | category | flops | bytes accessed | tf_op | source)
XLA Modules:
  0.0 106.5 jit_solution(4124850166775101476)
XLA Ops:
  0.6 0.8 slice_bitcast_fusion.1
  1.4 1.3 %pad_add_fusion.tab = s32[224]{0:T(256)} fusion(s32[32]{0:T(128)} %param.16, s32[64]{0:T(128)S(1)} %get-tuple-element.5, s32[64]{0:T(128)S(1)} %get-tuple-element.4, s32[64]{0:T(128)} %bitcast.5), kind=kLoop, calls=%fused_computation | loop fusion | flops 672 | bytes 1792 | tf_op jit(solution)/shard_map/concatenate | solution.py:517
  2.7 100.8 %shard_map.122 = (bf16[2,25,400]{2,1,0:T(8,128)(2,1)}, bf16[2,25,400]{2,1,0:T(8,128)(2,1)}) custom-call(s32[224]{0:T(256)} %pad_add_fusion.tab, bf16[1,20,256]{2,1,0:T(8,128)(2,1)} %val_any.1, bf16[1,20,256]{2,1,0:T(8,128)(2,1)} %con_any.1, bf16[1,256,4096]{2,1,0:T(8,128)(2,1)} %w_any.1, bf16[128,512]{1,0:T(8,128)(2,1)} %constant.10.clone.spread_d_any, ...), custom_call_target="tpu_custom_call" | custom-call | tf_op jit(solution)/shard_map/pallas_call | solution.py:553
  103.5 1.5 %copy.13 = bf16[2,25,400]{2,0,1:T(2,128)(2,1)} copy(bf16[2,25,400]{2,1,0:T(8,128)(2,1)} %get-tuple-element.2) | data formatting | bytes 80000 | tf_op jit(solution)/shard_map/pallas_call | solution.py:553
  105.0 1.5 %copy.14 = bf16[2,25,400]{2,0,1:T(2,128)(2,1)} copy(bf16[2,25,400]{2,1,0:T(8,128)(2,1)} %get-tuple-element.3) | data formatting | bytes 80000 | tf_op jit(solution)/shard_map/pallas_call | solution.py:553

commit v4 on v3

--- a/solution.py
+++ b/solution.py
@@ -17,6 +17,8 @@
 KB = 2 * BP
 CG = 4
 CW = NB // CG
+WIDE = CW * NB
+TAIL = WIDE // CG
 PAIR_DEV = 2
 MOST = 6
 HALF = MOST // 2
@@ -29,7 +31,7 @@
 
 def kernel(
     ny, nx, nz, pairs,
-    tab, val_any, con_any, w_any, spread_d_any, mask_d_any, spread_m_any, mask_m_any, collect_any,
+    tq, tp, to_slot, val_any, con_any, w_any, spread_d_any, mask_d_any, spread_m_any, mask_m_any, collect_any,
     out_d, out_m,
     val, con, w, spread_d, mask_d, spread_m, mask_m, collect,
     call, vall, g, acc, prod, valp, pf, pp, rr, rp, rm, sp, sm, yb, xs, xr_d, xr_m, ms, mr,
@@ -127,7 +129,7 @@
         for i in near:
             by(n, i).start()
 
-    pf[:, units * NB:, :] = jnp.zeros((rows, pf.shape[1] - units * NB, 128), F32)
+    pf[...] = jnp.zeros(pf.shape, F32)
 
     @pl.loop(0, MOST)
     def _(s):
@@ -137,21 +139,21 @@
         pass_on(0, i)
 
     def owner(k):
-        return tab[3 * pairs + k]
+        return to_slot[k]
 
     def own_slots(p, carry):
         count, slots = carry
-        hit = tab[p] == me
+        hit = tq[0, p] == me
         slots = tuple(jnp.where(hit & (count == s), p, slots[s]) for s in range(MOST))
         return count + hit.astype(jnp.int32), slots
 
     zero = jnp.int32(0)
     _, slots = lax.fori_loop(0, pairs, own_slots, (zero, (zero,) * MOST))
-    first = [owner(tab[pairs + p]) for p in slots]
-    second = [owner(tab[2 * pairs + p]) for p in slots]
+    first = [owner(tp[0, p]) for p in slots]
+    second = [owner(tp[1, p]) for p in slots]
 
     def by_second(p, carry):
-        e = owner(tab[2 * pairs + p])
+        e = owner(tp[1, p])
         new = []
         for k in range(nx):
             count, one, two = carry[k]
@@ -165,11 +167,11 @@
     for k in range(nx):
         at = (y * nx + k) * PAIR_DEV
         wanted += [at, at + 1, found[k][1], found[k][2]]
-    column = [tab[p] for p in wanted]
+    column = [tq[0, p] for p in wanted]
 
     def ranks(p, carry):
         return tuple(
-            n + ((tab[p] == q) & (p < own)).astype(jnp.int32) for n, q, own in zip(carry, column, wanted)
+            n + ((tq[0, p] == q) & (p < own)).astype(jnp.int32) for n, q, own in zip(carry, column, wanted)
         )
 
     ranked = lax.fori_loop(0, pairs, ranks, (zero,) * len(wanted))
@@ -210,23 +212,29 @@
             device_id=(y, x, z, 1 - c), device_id_type=MESH,
         )
 
-    def block(zz):
+    def block_slot(zz, s):
+        for core in range(2):
+            for h in range(2):
+                lane = (core * 2 + h) * 128
+                one = g[zz * 2 + core, s, h * BP:(h + 1) * BP, :]
+                two = g[zz * 2 + core, MOST + s, h * BP:(h + 1) * BP, :]
+                for k in range(NB):
+                    prod[k * BP:(k + 1) * BP, lane:lane + 128] = one[k:k + 1, :] * two
+        cols = pl.ds(pl.multiple_of(zz * 512, 512), 512)
+        acc[s] += lax.dot_general(
+            prod[...], w[:, cols], (((1,), (1,)), ((), ())), preferred_element_type=F32
+        )
+
+    def block_in(zz):
         for h in range(2):
             sibling(zz, 1 - c, h).wait_recv()
 
+    def block(zz):
+        block_in(zz)
+
         @pl.loop(0, MOST)
         def _(s):
-            for core in range(2):
-                for h in range(2):
-                    lane = (core * 2 + h) * 128
-                    one = g[zz * 2 + core, s, h * BP:(h + 1) * BP, :]
-                    two = g[zz * 2 + core, MOST + s, h * BP:(h + 1) * BP, :]
-                    for k in range(NB):
-                        prod[k * BP:(k + 1) * BP, lane:lane + 128] = one[k:k + 1, :] * two
-            cols = pl.ds(pl.multiple_of(zz * 512, 512), 512)
-            acc[s] += lax.dot_general(
-                prod[...], w[:, cols], (((1,), (1,)), ((), ())), preferred_element_type=F32
-            )
+            block_slot(zz, s)
 
     for h in range(CHUNKS):
         for d in (1, -1):
@@ -251,8 +259,6 @@
                 if half < len(before):
                     block(before[half])
         before = [zrel(-t), zrel(t)] if t < top else [zrel(t)]
-    for zz in before:
-        block(zz)
     all_arrived(1)
 
     def pair_copy(s):
@@ -277,7 +283,13 @@
             for v in range(NB):
                 u = v * CG + q
                 r, i = u // units, u % units
-                pf[r, i * NB:(i + 1) * NB, :] = part[v * BP:v * BP + NB, :]
+                piece = part[v * BP:(v + 1) * BP, :]
+                if i < CG:
+                    pf[r, i * NB:(i + 1) * NB, :WIDE] = piece[:NB, :WIDE]
+                else:
+                    for k in range(CG):
+                        moved = pltpu.roll(piece, WIDE - k * TAIL, 1)
+                        pf[r, k * NB:(k + 1) * NB, WIDE:WIDE + TAIL] = moved[:NB, WIDE:WIDE + TAIL]
         for r in range(rows):
             pp[s, r % 2, r // 2] = pf[r].astype(BF)
         pair_copy(s).start()
@@ -352,7 +364,12 @@
                     ysend(d, t + 1, s).start()
 
     for s in range(MOST + 1):
+        if s == 0:
+            for zz in before:
+                block_in(zz)
         if s < MOST:
+            for zz in before:
+                block_slot(zz, s)
             partial(s)
         if s:
             added(s - 1)
@@ -392,12 +409,18 @@
     for i in range(1, nx):
         xcopy(i, 1).wait_recv()
 
-    srows = xs.shape[2]
+    srows = mask_d.shape[0]
     at_r = lax.broadcasted_iota(jnp.int32, (srows, 128), 0)
     at_l = lax.broadcasted_iota(jnp.int32, (srows, 128), 1)
 
     def ordered(m, j, spread, mask):
-        got = (xr_d, xr_m)[m][loc_t[8 * nx + x * 4 + m * PAIR_DEV + j], j].astype(F32)
+        base = (xr_d, xr_m)[m][loc_t[8 * nx + x * 4 + m * PAIR_DEV + j], j].astype(F32)
+        last = jnp.zeros((NB, 128), F32)
+        lane = lax.broadcasted_iota(jnp.int32, (NB, 128), 1)
+        for k in range(CG):
+            moved = pltpu.roll(base[k * NB:(k + 1) * NB, :], 128 - (WIDE - k * TAIL), 1)
+            last = jnp.where((lane >= k * TAIL) & (lane < (k + 1) * TAIL), moved, last)
+        got = jnp.concatenate([base, last, jnp.zeros((srows - units * NB, 128), F32)], axis=0)
         kept = [
             jnp.where((at_r < units * NB) & (at_l >= k * NB) & (at_l < (k + 1) * NB), got, 0.0).astype(BF)
             for k in range(CW)
@@ -430,17 +453,19 @@
 
     for i in range(1, nx):
         xcopy(i, 0).wait_recv()
-    for j in range(PAIR_DEV):
-        out_d[j] = ordered(0, j, spread_d, mask_d)[:share, :NB * NB].astype(BF)
+    out_d[...] = jnp.stack(
+        [ordered(0, j, spread_d, mask_d)[:share, :NB * NB] for j in range(PAIR_DEV)], axis=1
+    ).astype(BF)
 
     @pl.loop(1, rows)
     def _(i):
         mcopy(i).wait_recv()
 
-    for j in range(PAIR_DEV):
-        out_m[j] = jnp.concatenate(
+    out_m[...] = jnp.stack([
+        jnp.concatenate(
             [mr[r].astype(F32)[:share, j * rpad:j * rpad + share] for r in range(rows)], axis=1
-        ).astype(BF)
+        ) for j in range(PAIR_DEV)
+    ], axis=1).astype(BF)
 
     for n in range(2):
         for i in range(ny):
@@ -514,11 +539,10 @@
 
     def shards(val, con, screened, pair_list, transfer_index, owner_map):
         pairs = pair_list.shape[0]
-        tab = jnp.concatenate([transfer_index[:, 0], pair_list[:, 0], pair_list[:, 1], owner_map])
         consts = [jnp.asarray(a) for a in constants(rows)]
         vmem, anywhere = pl.BlockSpec(memory_space=pltpu.VMEM), pl.BlockSpec(memory_space=pl.ANY)
         points = screened.shape[2]
-        blk = (srows, 128)
+        blk = ((units - 1) * NB, 128)
         scratch = [
             pltpu.VMEM(val.shape, BF), pltpu.VMEM(con.shape, BF),
             pltpu.VMEM((256, points), BF),
@@ -549,17 +573,18 @@
             *[dma((ytop, MOST)) for _ in range(4)],
             dma((2, nx)), dma((2, nx)), dma((rows,)), dma((rows,)),
         ]
-        result = jax.ShapeDtypeStruct((PAIR_DEV, share, NB * NB), BF)
-        return pl.pallas_call(
+        result = jax.ShapeDtypeStruct((share, PAIR_DEV, NB * NB), BF)
+        direct, mirror = pl.pallas_call(
             functools.partial(kernel, ny, nx, nz, pairs),
             out_shape=(result, result),
-            in_specs=[pl.BlockSpec(memory_space=pltpu.SMEM), *[anywhere] * 8],
+            in_specs=[*[pl.BlockSpec(memory_space=pltpu.SMEM)] * 3, *[anywhere] * 8],
             out_specs=(vmem, vmem),
             scratch_shapes=scratch,
             compiler_params=pltpu.CompilerParams(
                 collective_id=0, has_side_effects=True, vmem_limit_bytes=60 * 2**20
             ),
-        )(tab, val, con, screened, *consts)
+        )(transfer_index.T, pair_list.T, owner_map, val, con, screened, *consts)
+        return direct.transpose(1, 0, 2), mirror.transpose(1, 0, 2)
 
     in_specs = (P(("y", "x"), None, ("z", "c")), P(("y", "x"), None, ("z", "c")),
                 P(("y", "x"), ("z", "c"), None), P(), P(), P())

time: 107 us -> 101 us (0.944)
  Pallas kernels: 101 us -> 97.4 us
  other arithmetic: 1.31 us -> 0 us
    pallas_call x1, Pallas kernels: 101 us -> 97.4 us  [shards(): pl.pallas_call(functools.partial(kernel, ny, nx, nz, pairs), out_shape=(r...]
    pallas_call x2 -> x0, local copies, waits for them, and re-layouts: 3.03 us -> none  [shards(): pl.pallas_call(functools.partial(kernel, ny, nx, nz, pairs), out_shape=(r...]
    unnamed x0 -> x2, local copies, waits for them, and re-layouts: none -> 2.92 us
    concatenate x1 -> x0, other arithmetic: 1.31 us -> none  [shards(): jnp.concatenate([transfer_index[:, 0], pair_list[:, 0], pair_list[:, 1],...]
where the time goes in v4:
time: 101 us
  Pallas kernels  97.4 us (96%)
  local copies, waits for them, and re-layouts  2.92 us (3%)
    pallas_call x1, Pallas kernels, shards(): pl.pallas_call(functools.partial(kernel, ny, nx, nz, pairs), out_shape=(r...  97.4 us
    unnamed x2, local copies, waits for them, and re-layouts  2.92 us

profile of v4, /device:TPU:1, one launch (start us, length us, event | category | flops | bytes accessed | tf_op | source)
XLA Modules:
  0.0 101.0 jit_solution(3412298710153365423)
XLA Ops:
  0.6 97.4 %shard_map.122 = (bf16[25,2,400]{2,1,0:T(2,128)(2,1)}, bf16[25,2,400]{2,1,0:T(2,128)(2,1)}) custom-call(s32[1,64]{1,0:T(1,128)} %bitcast.7, s32[2,64]{1,0:T(2,128)} %bitcast.6, s32[32]{0:T(128)} %to_slot.1, bf16[1,20,256]{2,1,0:T(8,128)(2,1)} %val_any.1, bf16[1,20,256]{2,1,0:T(8,128)(2,1)} %con_any.1, bf16[1,256,4096]{2,1,0:T(8,128)(2,1)} %w_any.1, ...), custom_call_target="tpu_custom_call" | custom-call | tf_op jit(solution)/shard_map/pallas_call | solution.py:577
  98.0 1.5 %copy.15 = bf16[2,25,400]{2,0,1:T(2,128)(2,1)} copy(bf16[2,25,400]{2,0,1:T(2,128)(2,1)} %bitcast.5) | data formatting | bytes 80000
  99.5 1.5 %copy.16 = bf16[2,25,400]{2,0,1:T(2,128)(2,1)} copy(bf16[2,25,400]{2,0,1:T(2,128)(2,1)} %bitcast.4) | data formatting | bytes 80000

commit v5 on v4

--- a/solution.py
+++ b/solution.py
@@ -34,7 +34,7 @@
     tq, tp, to_slot, val_any, con_any, w_any, spread_d_any, mask_d_any, spread_m_any, mask_m_any, collect_any,
     out_d, out_m,
     val, con, w, spread_d, mask_d, spread_m, mask_m, collect,
-    call, vall, g, acc, prod, valp, pf, pp, rr, rp, rm, sp, sm, yb, xs, xr_d, xr_m, ms, mr,
+    wt, call, vall, g, acc, prod, valp, pf, pp, rr, rp, rm, sp, sm, yb, xs, xr_d, xr_m, ms, mr,
     loc_t, loc,
     by_s, by_r, bx_s, bx_r,
     gs_p, gr_p, gs_m, gr_m, ss_s, ss_r,
@@ -138,6 +138,10 @@
     for i in near:
         pass_on(0, i)
 
+    fetch[2].wait()
+    for zz in range(nz):
+        wt[zz] = w[:, zz * 512:(zz + 1) * 512].T
+
     def owner(k):
         return to_slot[k]
 
@@ -212,29 +216,24 @@
             device_id=(y, x, z, 1 - c), device_id_type=MESH,
         )
 
-    def block_slot(zz, s):
-        for core in range(2):
-            for h in range(2):
-                lane = (core * 2 + h) * 128
-                one = g[zz * 2 + core, s, h * BP:(h + 1) * BP, :]
-                two = g[zz * 2 + core, MOST + s, h * BP:(h + 1) * BP, :]
-                for k in range(NB):
-                    prod[k * BP:(k + 1) * BP, lane:lane + 128] = one[k:k + 1, :] * two
-        cols = pl.ds(pl.multiple_of(zz * 512, 512), 512)
-        acc[s] += lax.dot_general(
-            prod[...], w[:, cols], (((1,), (1,)), ((), ())), preferred_element_type=F32
-        )
-
     def block_in(zz):
         for h in range(2):
             sibling(zz, 1 - c, h).wait_recv()
 
-    def block(zz):
-        block_in(zz)
-
-        @pl.loop(0, MOST)
-        def _(s):
-            block_slot(zz, s)
+    def block_half(zz, a):
+        @pl.loop(0, HALF)
+        def _(i):
+            s = a * HALF + i
+            for core in range(2):
+                for h in range(2):
+                    lane = (core * 2 + h) * 128
+                    one = g[zz * 2 + core, s, h * BP:(h + 1) * BP, :]
+                    two = g[zz * 2 + core, MOST + s, h * BP:(h + 1) * BP, :]
+                    for k in range(NB):
+                        prod[i, k * BP:(k + 1) * BP, lane:lane + 128] = one[k:k + 1, :] * two
+        part = pl.ds(a * HALF, HALF)
+        some = jnp.dot(prod[...].reshape(HALF * NB * BP, 512), wt[zz], preferred_element_type=F32)
+        acc[part] += some.reshape(HALF, NB * BP, 256)
 
     for h in range(CHUNKS):
         for d in (1, -1):
@@ -242,7 +241,6 @@
                 gsend(d, 1, h).start()
     for h in range(2):
         sibling(z, c, h).start()
-    fetch[2].wait()
     before = [z]
     for t in range(1, top + 1):
         for h in range(CHUNKS):
@@ -256,8 +254,11 @@
                 for d in (1, -1):
                     if g_has(d, t, h):
                         sibling(zrel(-d * t), c, half).start()
-                if half < len(before):
-                    block(before[half])
+            piece = h * 4 // CHUNKS
+            if h % (CHUNKS // 4) == 0 and piece // 2 < len(before):
+                if piece % 2 == 0:
+                    block_in(before[piece // 2])
+                block_half(before[piece // 2], piece % 2)
         before = [zrel(-t), zrel(t)] if t < top else [zrel(t)]
     all_arrived(1)
 
@@ -368,8 +369,9 @@
             for zz in before:
                 block_in(zz)
         if s < MOST:
-            for zz in before:
-                block_slot(zz, s)
+            if s % HALF == 0:
+                for zz in before:
+                    block_half(zz, s // HALF)
             partial(s)
         if s:
             added(s - 1)
@@ -547,11 +549,12 @@
             pltpu.VMEM(val.shape, BF), pltpu.VMEM(con.shape, BF),
             pltpu.VMEM((256, points), BF),
             *[pltpu.VMEM(a.shape, BF) for a in consts],
+            pltpu.VMEM((nz, 512, 256), BF),
             pltpu.VMEM((ny, nx, KB, 128), BF),
             pltpu.VMEM((ny, nx, KB, 128), BF),
             pltpu.VMEM((rows, 2 * MOST, KB, 128), BF),
             pltpu.VMEM((MOST, NB * BP, 256), F32),
-            pltpu.VMEM((NB * BP, 512), BF),
+            pltpu.VMEM((HALF, NB * BP, 512), BF),
             pltpu.VMEM((NB * BP, 256), BF),
             pltpu.VMEM((rows, *blk), F32),
             pltpu.VMEM((MOST, 2, nz, *blk), BF),

time: 101 us -> 105 us (1.040)
  Pallas kernels: 97.4 us -> 101 us
    pallas_call x1, Pallas kernels: 97.4 us -> 101 us  [shards(): pl.pallas_call(functools.partial(kernel, ny, nx, nz, pairs), out_shape=(r...]
where the time goes in v5:
time: 105 us; the launch traced here: 104 us
  Pallas kernels  101 us (96%)
  local copies, waits for them, and re-layouts  2.92 us (3%)
    pallas_call x1, Pallas kernels, shards(): pl.pallas_call(functools.partial(kernel, ny, nx, nz, pairs), out_shape=(r...  101 us
    unnamed x2, local copies, waits for them, and re-layouts  2.92 us

profile of v5, /device:TPU:1, one launch (start us, length us, event | category | flops | bytes accessed | tf_op | source)
XLA Modules:
  0.0 104.3 jit_solution(11168651756936596114)
XLA Ops:
  0.6 100.8 %shard_map.122 = (bf16[25,2,400]{2,1,0:T(2,128)(2,1)}, bf16[25,2,400]{2,1,0:T(2,128)(2,1)}) custom-call(s32[1,64]{1,0:T(1,128)} %bitcast.7, s32[2,64]{1,0:T(2,128)} %bitcast.6, s32[32]{0:T(128)} %to_slot.1, bf16[1,20,256]{2,1,0:T(8,128)(2,1)} %val_any.1, bf16[1,20,256]{2,1,0:T(8,128)(2,1)} %con_any.1, bf16[1,256,4096]{2,1,0:T(8,128)(2,1)} %w_any.1, ...), custom_call_target="tpu_custom_call" | custom-call | tf_op jit(solution)/shard_map/pallas_call | solution.py:580
  101.4 1.5 %copy.15 = bf16[2,25,400]{2,0,1:T(2,128)(2,1)} copy(bf16[2,25,400]{2,0,1:T(2,128)(2,1)} %bitcast.5) | data formatting | bytes 80000
  102.9 1.5 %copy.16 = bf16[2,25,400]{2,0,1:T(2,128)(2,1)} copy(bf16[2,25,400]{2,0,1:T(2,128)(2,1)} %bitcast.4) | data formatting | bytes 80000

commit v6 on v4

--- a/solution.py
+++ b/solution.py
@@ -34,7 +34,7 @@
     tq, tp, to_slot, val_any, con_any, w_any, spread_d_any, mask_d_any, spread_m_any, mask_m_any, collect_any,
     out_d, out_m,
     val, con, w, spread_d, mask_d, spread_m, mask_m, collect,
-    call, vall, g, acc, prod, valp, pf, pp, rr, rp, rm, sp, sm, yb, xs, xr_d, xr_m, ms, mr,
+    wt, call, vall, g, acc, prod, valp, pf, pp, rr, rp, rm, sp, sm, yb, xs, xr_d, xr_m, ms, mr,
     loc_t, loc,
     by_s, by_r, bx_s, bx_r,
     gs_p, gr_p, gs_m, gr_m, ss_s, ss_r,
@@ -138,6 +138,10 @@
     for i in near:
         pass_on(0, i)
 
+    fetch[2].wait()
+    for zz in range(nz):
+        wt[zz] = w[:, zz * 512:(zz + 1) * 512].T
+
     def owner(k):
         return to_slot[k]
 
@@ -220,10 +224,7 @@
                 two = g[zz * 2 + core, MOST + s, h * BP:(h + 1) * BP, :]
                 for k in range(NB):
                     prod[k * BP:(k + 1) * BP, lane:lane + 128] = one[k:k + 1, :] * two
-        cols = pl.ds(pl.multiple_of(zz * 512, 512), 512)
-        acc[s] += lax.dot_general(
-            prod[...], w[:, cols], (((1,), (1,)), ((), ())), preferred_element_type=F32
-        )
+        acc[s] += jnp.dot(prod[...], wt[zz], preferred_element_type=F32)
 
     def block_in(zz):
         for h in range(2):
@@ -242,7 +243,6 @@
                 gsend(d, 1, h).start()
     for h in range(2):
         sibling(z, c, h).start()
-    fetch[2].wait()
     before = [z]
     for t in range(1, top + 1):
         for h in range(CHUNKS):
@@ -547,6 +547,7 @@
             pltpu.VMEM(val.shape, BF), pltpu.VMEM(con.shape, BF),
             pltpu.VMEM((256, points), BF),
             *[pltpu.VMEM(a.shape, BF) for a in consts],
+            pltpu.VMEM((nz, 512, 256), BF),
             pltpu.VMEM((ny, nx, KB, 128), BF),
             pltpu.VMEM((ny, nx, KB, 128), BF),
             pltpu.VMEM((rows, 2 * MOST, KB, 128), BF),

time: 101 us -> 103 us (1.020)
  Pallas kernels: 97.4 us -> 99.2 us
    pallas_call x1, Pallas kernels: 97.4 us -> 99.2 us  [shards(): pl.pallas_call(functools.partial(kernel, ny, nx, nz, pairs), out_shape=(r...]
where the time goes in v6:
time: 103 us
  Pallas kernels  99.2 us (96%)
  local copies, waits for them, and re-layouts  2.92 us (3%)
    pallas_call x1, Pallas kernels, shards(): pl.pallas_call(functools.partial(kernel, ny, nx, nz, pairs), out_shape=(r...  99.2 us
    unnamed x2, local copies, waits for them, and re-layouts  2.92 us

profile of v6, /device:TPU:1, one launch (start us, length us, event | category | flops | bytes accessed | tf_op | source)
XLA Modules:
  0.0 102.8 jit_solution(1233723055577429650)
XLA Ops:
  0.6 99.2 %shard_map.122 = (bf16[25,2,400]{2,1,0:T(2,128)(2,1)}, bf16[25,2,400]{2,1,0:T(2,128)(2,1)}) custom-call(s32[1,64]{1,0:T(1,128)} %bitcast.7, s32[2,64]{1,0:T(2,128)} %bitcast.6, s32[32]{0:T(128)} %to_slot.1, bf16[1,20,256]{2,1,0:T(8,128)(2,1)} %val_any.1, bf16[1,20,256]{2,1,0:T(8,128)(2,1)} %con_any.1, bf16[1,256,4096]{2,1,0:T(8,128)(2,1)} %w_any.1, ...), custom_call_target="tpu_custom_call" | custom-call | tf_op jit(solution)/shard_map/pallas_call | solution.py:578
  99.8 1.5 %copy.15 = bf16[2,25,400]{2,0,1:T(2,128)(2,1)} copy(bf16[2,25,400]{2,0,1:T(2,128)(2,1)} %bitcast.5) | data formatting | bytes 80000
  101.3 1.5 %copy.16 = bf16[2,25,400]{2,0,1:T(2,128)(2,1)} copy(bf16[2,25,400]{2,0,1:T(2,128)(2,1)} %bitcast.4) | data formatting | bytes 80000

commit v7 on v4

--- a/solution.py
+++ b/solution.py
@@ -22,7 +22,7 @@
 PAIR_DEV = 2
 MOST = 6
 HALF = MOST // 2
-CHUNKS = 4
+CHUNKS = 2
 
 
 def up(n, to):

time: 101 us -> 101 us (level)
  no operation moved by 1% of the time
where the time goes in v7:
time: 101 us
  Pallas kernels  97.6 us (97%)
  local copies, waits for them, and re-layouts  2.92 us (3%)
    pallas_call x1, Pallas kernels, shards(): pl.pallas_call(functools.partial(kernel, ny, nx, nz, pairs), out_shape=(r...  97.6 us
    unnamed x2, local copies, waits for them, and re-layouts  2.92 us

profile of v7, /device:TPU:1, one launch (start us, length us, event | category | flops | bytes accessed | tf_op | source)
XLA Modules:
  0.0 101.1 jit_solution(13596104438856314344)
XLA Ops:
  0.6 97.6 %shard_map.122 = (bf16[25,2,400]{2,1,0:T(2,128)(2,1)}, bf16[25,2,400]{2,1,0:T(2,128)(2,1)}) custom-call(s32[1,64]{1,0:T(1,128)} %bitcast.7, s32[2,64]{1,0:T(2,128)} %bitcast.6, s32[32]{0:T(128)} %to_slot.1, bf16[1,20,256]{2,1,0:T(8,128)(2,1)} %val_any.1, bf16[1,20,256]{2,1,0:T(8,128)(2,1)} %con_any.1, bf16[1,256,4096]{2,1,0:T(8,128)(2,1)} %w_any.1, ...), custom_call_target="tpu_custom_call" | custom-call | tf_op jit(solution)/shard_map/pallas_call | solution.py:577
  98.2 1.5 %copy.15 = bf16[2,25,400]{2,0,1:T(2,128)(2,1)} copy(bf16[2,25,400]{2,0,1:T(2,128)(2,1)} %bitcast.5) | data formatting | bytes 80000
  99.7 1.5 %copy.16 = bf16[2,25,400]{2,0,1:T(2,128)(2,1)} copy(bf16[2,25,400]{2,0,1:T(2,128)(2,1)} %bitcast.4) | data formatting | bytes 80000
